TPU v7x, 32 devices: a whole 2x2x4 slice. The times are simulated.
32 devices in a mesh: dp: 8 (over z, x), tensor: 4 (over y, core).
Axes of the slice: x: 2, y: 2, z: 4, core: 2. Of those that a mesh axis runs over, the one named last changes fastest.
Arguments:
- query_stream: bfloat16 [4, 8192, 512], P(None, 'dp'), may hold values from -6 to 6
- context_stream: bfloat16 [4, 8192, 512], P(None, 'dp'), may hold values from -6 to 6
- encoder_out: bfloat16 [4, 8192, 512], P(None, 'dp'), may hold values from -6 to 6
- query_masks: int32 [4, 4096, 128], P(None, 'dp'), may hold values from 0 to 1, as said below
- source_segments: int32 [4, 8, 1024], P(None, 'dp'), may hold values from 0 to 15, never falling along the last dimension, each value on 1 to 128 neighbouring positions
- out_grad: bfloat16 [4, 8192, 512], P(None, ('dp', 'tensor')), may hold values from -6 to 6
- self_query: bfloat16 [512, 512], P('dp', 'tensor'), may hold values from -0.25 to 0.25
- self_key_value: bfloat16 [2, 512, 512], P(None, 'dp', 'tensor'), may hold values from -0.25 to 0.25
- self_output: bfloat16 [512, 512], P('tensor', 'dp'), may hold values from -1.5 to 1.5
- cross_query: bfloat16 [512, 512], P('dp', 'tensor'), may hold values from -0.25 to 0.25
- cross_key_value: bfloat16 [2, 512, 512], P(None, 'dp', 'tensor'), may hold values from -0.25 to 0.25
- cross_output: bfloat16 [512, 512], P('tensor', 'dp'), may hold values from -2 to 2
- ffn_in: bfloat16 [512, 2048], P('dp'), may hold values from -0.25 to 0.25
- ffn_out: bfloat16 [2048, 512], P('dp'), may hold values from -0.1875 to 0.1875
- norm_gain: bfloat16 [3, 512], P(None, 'dp'), may hold values from 0.5 to 1.5
- norm_bias: bfloat16 [3, 512], P(None, 'dp'), may hold values from -3 to 3
Outputs:
- block_out: bfloat16 [4, 8192, 512], P(None, ('dp', 'tensor'))
- stream_grad: bfloat16 [4, 8192, 512], P(None, ('dp', 'tensor'))
- context_grad: bfloat16 [4, 8192, 512], P(None, ('dp', 'tensor'))
- encoder_grad: bfloat16 [4, 8192, 512], P(None, ('dp', 'tensor'))
- grad_self_query: float32 [512, 512], P('dp', 'tensor')
- grad_self_key_value: float32 [2, 512, 512], P(None, 'dp', 'tensor')
- grad_self_output: float32 [512, 512], P('tensor', 'dp')
- grad_cross_query: float32 [512, 512], P('dp', 'tensor')
- grad_cross_key_value: float32 [2, 512, 512], P(None, 'dp', 'tensor')
- grad_cross_output: float32 [512, 512], P('tensor', 'dp')
- grad_ffn_in: float32 [512, 2048], P('dp')
- grad_ffn_out: float32 [2048, 512], P('dp')
- grad_norm_gain: float32 [3, 512], P(None, 'dp')
- grad_norm_bias: float32 [3, 512], P(None, 'dp')
Inputs may be any that keep to these rules, and one draw needn't show every extreme that they name: `query_masks`: token t of a micro-batch owns entries t * 64 to t * 64 + 63 of the flattened array, one for each position of its slot; the entry of its own position is 0 and at least one entry is 1. `source_segments`: along a row the numbers never fall, and every slot number has 1 to 128 encoder tokens, one exactly 128.
All inputs are finite; a program needn't handle non-finite values.
Results may differ from a plain program's by a relative error of at most 0.034.
Values may be sent and summed in bfloat16 or wider, within the bound.
A program may use at most 192 MiB of HBM per device.

v0:
```python
import jax
import jax.numpy as jnp
from jax import lax
from jax.sharding import PartitionSpec as P

HEAD_DIM = 64
SLOT = 64
SEG_MOST = 128


epsilon = 1e-05
neg_fill = -1e30
gelu_coef = 0.7978845608028654
gelu_cube = 0.044715


def smooth_gate(value):
    return 0.5 * value * (1.0 + jnp.tanh(gelu_coef * (value + gelu_cube * value * value * value)))


def smooth_slope(value):
    bent = jnp.tanh(gelu_coef * (value + gelu_cube * value * value * value))
    return 0.5 * (1.0 + bent) + 0.5 * value * (1.0 - bent * bent) * gelu_coef * (
        1.0 + 3.0 * gelu_cube * value * value
    )


def norm_forward(value, gain, bias):
    center = jnp.mean(value, axis=-1, keepdims=True)
    shifted = value - center
    factor = lax.rsqrt(jnp.mean(shifted * shifted, axis=-1, keepdims=True) + epsilon)
    normed = shifted * factor
    return (normed * gain + bias, normed, factor)


def norm_backward(incoming, normed, factor, gain):
    scaled = incoming * gain
    inside = (
        scaled
        - jnp.mean(scaled, axis=-1, keepdims=True)
        - normed * jnp.mean(scaled * normed, axis=-1, keepdims=True)
    )
    return (factor * inside, jnp.sum(incoming * normed, axis=0), jnp.sum(incoming, axis=0))


def scores_of(queries, key_rows, allowed):
    raw = jnp.einsum(
        "nqhe,nkhe->nhqk", queries, key_rows, preferred_element_type=jnp.float32
    ) * HEAD_DIM ** (-0.5)
    return jnp.where(allowed[:, None], raw, neg_fill)


def attend_core(queries, key_rows, value_rows, allowed):
    scores = scores_of(queries, key_rows, allowed)
    row_top = jnp.max(scores, axis=-1, keepdims=True)
    summed = jnp.sum(jnp.exp(scores - row_top), axis=-1, keepdims=True)
    log_total = row_top + jnp.log(summed)
    probs = jnp.exp(scores - log_total).astype(jnp.bfloat16)
    mixed = jnp.einsum("nhqk,nkhe->nqhe", probs, value_rows, preferred_element_type=jnp.float32)
    return (mixed.astype(jnp.bfloat16), log_total)


def attend_back_core(queries, key_rows, value_rows, allowed, log_total, d_mixed):
    scores = scores_of(queries, key_rows, allowed)
    probs = jnp.exp(scores - log_total)
    d_probs = jnp.einsum("nqhe,nkhe->nhqk", d_mixed, value_rows, preferred_element_type=jnp.float32)
    inner_sum = jnp.sum(probs * d_probs, axis=-1, keepdims=True)
    d_scores = (probs * (d_probs - inner_sum)).astype(jnp.bfloat16)
    factor = HEAD_DIM ** (-0.5)
    d_queries = (
        jnp.einsum("nhqk,nkhe->nqhe", d_scores, key_rows, preferred_element_type=jnp.float32)
        * factor
    ).astype(jnp.bfloat16)
    d_keys = (
        jnp.einsum("nhqk,nqhe->nkhe", d_scores, queries, preferred_element_type=jnp.float32)
        * factor
    )
    d_values = jnp.einsum(
        "nhqk,nqhe->nkhe", probs.astype(jnp.bfloat16), d_mixed, preferred_element_type=jnp.float32
    )
    return (d_queries, d_keys, d_values)


def self_one(operands):
    queries, key_rows, value_rows, allowed = operands
    return attend_core(queries, key_rows, value_rows, allowed)


def self_back_one(operands):
    queries, key_rows, value_rows, allowed, log_total, d_mixed = operands
    d_queries, d_keys, d_values = attend_back_core(
        queries, key_rows, value_rows, allowed, log_total, d_mixed
    )
    return (d_queries, d_keys.astype(jnp.bfloat16), d_values.astype(jnp.bfloat16))


def window_of(rows, starts):
    blocks = rows.reshape((rows.shape[0] // SEG_MOST, SEG_MOST) + rows.shape[1:])
    return jnp.concatenate([blocks[starts], blocks[starts + 1]], axis=1)


def window_allowed(segments, starts, query_count):
    seg_window = window_of(segments, starts)
    slot_index = jnp.arange(starts.shape[0], dtype=jnp.int32)
    allowed = seg_window == slot_index[:, None]
    return jnp.broadcast_to(
        allowed[:, None, :], (starts.shape[0], query_count, seg_window.shape[1])
    )


def fold_window(grads, starts, length):
    block_total = length // SEG_MOST
    pieces = jnp.concatenate([grads[:, :SEG_MOST], grads[:, SEG_MOST:]], axis=0)
    targets = jnp.concatenate([starts, starts + 1], axis=0)
    summed = jax.ops.segment_sum(pieces, targets, num_segments=block_total)
    return summed.reshape((length,) + grads.shape[2:]).astype(jnp.bfloat16)


def cross_one(operands):
    queries, key_rows, value_rows, starts, segments = operands
    allowed = window_allowed(segments, starts, queries.shape[1])
    return attend_core(queries, window_of(key_rows, starts), window_of(value_rows, starts), allowed)


def cross_back_one(operands):
    queries, key_rows, value_rows, starts, segments, log_total, d_mixed = operands
    allowed = window_allowed(segments, starts, queries.shape[1])
    d_queries, d_keys, d_values = attend_back_core(
        queries,
        window_of(key_rows, starts),
        window_of(value_rows, starts),
        allowed,
        log_total,
        d_mixed,
    )
    return (
        d_queries,
        fold_window(d_keys, starts, key_rows.shape[0]),
        fold_window(d_values, starts, key_rows.shape[0]),
    )


def weight_grad(left, right):
    return jnp.einsum("td,te->de", left, right, preferred_element_type=jnp.float32)


def back_project(gradient, weight):
    return jnp.einsum("te,de->td", gradient, weight, preferred_element_type=jnp.float32)


def micro_step(
    weights, stream_full, stream_part, context, source, cotangent, bits, segments, reducers
):
    w_query, w_pair, w_out, c_query, c_pair, c_out, f_in, f_out, gains, biases = weights
    mix_self, spread_first, mix_cross, spread_second, back_cross, spread_third, back_self = reducers
    gains = gains.astype(jnp.float32)
    biases = biases.astype(jnp.float32)
    tokens = stream_full.shape[0]
    row_count, enc_length = segments.shape
    row_length = tokens // row_count
    block_size = min(512, row_length)
    block_count = tokens // block_size
    pair_size = 2 * SLOT
    pair_count = block_size // pair_size
    slot_count = row_length // SLOT
    local_heads = w_query.shape[1] // HEAD_DIM
    head_width = local_heads * HEAD_DIM
    self_shape = (block_count, pair_count, pair_size, local_heads, HEAD_DIM)
    cross_shape = (row_count, slot_count, SLOT, local_heads, HEAD_DIM)
    pair_slot = jnp.arange(pair_size, dtype=jnp.int32) // SLOT
    seen = jnp.tile(bits.reshape(block_count, pair_count, pair_size, SLOT), (1, 1, 1, 2)) == 1
    allowed_self = seen & (pair_slot[:, None] == pair_slot[None, :])
    slot_index = jnp.arange(slot_count, dtype=jnp.int32)
    first_place = jnp.sum(
        (segments[:, None, :] < slot_index[None, :, None]).astype(jnp.int32), axis=-1
    )
    starts = jnp.minimum(first_place // SEG_MOST, enc_length // SEG_MOST - 2)
    query_self = jnp.dot(stream_full, w_query, preferred_element_type=jnp.float32).astype(
        jnp.bfloat16
    )
    query_self = query_self.reshape(self_shape)
    pair_self = jnp.einsum(
        "td,kde->kte", context, w_pair, preferred_element_type=jnp.float32
    ).astype(jnp.bfloat16)
    key_self = pair_self[0].reshape(self_shape)
    value_self = pair_self[1].reshape(self_shape)
    mixed_self, total_self = lax.map(self_one, (query_self, key_self, value_self, allowed_self))
    mixed_self = mixed_self.reshape(tokens, head_width)
    attn_self = mix_self(mixed_self, w_out)
    first, normed_first, factor_first = norm_forward(
        stream_part.astype(jnp.float32) + attn_self, gains[0], biases[0]
    )
    first_full = spread_first(first.astype(jnp.bfloat16))
    query_cross = jnp.dot(first_full, c_query, preferred_element_type=jnp.float32).astype(
        jnp.bfloat16
    )
    query_cross = query_cross.reshape(cross_shape)
    pair_cross = jnp.einsum(
        "td,kde->kte", source, c_pair, preferred_element_type=jnp.float32
    ).astype(jnp.bfloat16)
    key_cross = pair_cross[0].reshape(row_count, enc_length, local_heads, HEAD_DIM)
    value_cross = pair_cross[1].reshape(row_count, enc_length, local_heads, HEAD_DIM)
    mixed_cross, total_cross = lax.map(
        cross_one, (query_cross, key_cross, value_cross, starts, segments)
    )
    mixed_cross = mixed_cross.reshape(tokens, head_width)
    attn_cross = mix_cross(mixed_cross, c_out)
    second, normed_second, factor_second = norm_forward(first + attn_cross, gains[1], biases[1])
    second_low = second.astype(jnp.bfloat16)
    inner = jnp.dot(second_low, f_in, preferred_element_type=jnp.float32)
    hidden = smooth_gate(inner).astype(jnp.bfloat16)
    ffn_value = jnp.dot(hidden, f_out, preferred_element_type=jnp.float32)
    result, normed_third, factor_third = norm_forward(second + ffn_value, gains[2], biases[2])
    d_third, gain_third, bias_third = norm_backward(
        cotangent.astype(jnp.float32), normed_third, factor_third, gains[2]
    )
    d_ffn = d_third.astype(jnp.bfloat16)
    grad_f_out = weight_grad(hidden, d_ffn)
    d_hidden = back_project(d_ffn, f_out)
    d_inner = (d_hidden * smooth_slope(inner)).astype(jnp.bfloat16)
    grad_f_in = weight_grad(second_low, d_inner)
    d_second = d_third + back_project(d_inner, f_in)
    d_cross, gain_second, bias_second = norm_backward(
        d_second, normed_second, factor_second, gains[1]
    )
    d_cross_full = spread_second(d_cross.astype(jnp.bfloat16))
    grad_c_out = weight_grad(mixed_cross, d_cross_full)
    d_mixed_cross = back_project(d_cross_full, c_out).astype(jnp.bfloat16)
    d_mixed_cross = d_mixed_cross.reshape(cross_shape)
    dq_cross, dk_cross, dv_cross = lax.map(
        cross_back_one,
        (query_cross, key_cross, value_cross, starts, segments, total_cross, d_mixed_cross),
    )
    dq_cross = dq_cross.reshape(tokens, head_width)
    dk_cross = dk_cross.reshape(row_count * enc_length, head_width)
    dv_cross = dv_cross.reshape(row_count * enc_length, head_width)
    grad_c_query = weight_grad(first_full, dq_cross)
    grad_c_pair = jnp.stack([weight_grad(source, dk_cross), weight_grad(source, dv_cross)])
    first_term = back_project(dq_cross, c_query)
    source_term = back_project(dk_cross, c_pair[0]) + back_project(dv_cross, c_pair[1])
    first_summed, source_summed = back_cross((first_term, source_term))
    d_first = d_cross + first_summed
    d_attn, gain_first, bias_first = norm_backward(d_first, normed_first, factor_first, gains[0])
    d_attn_full = spread_third(d_attn.astype(jnp.bfloat16))
    grad_w_out = weight_grad(mixed_self, d_attn_full)
    d_mixed_self = back_project(d_attn_full, w_out).astype(jnp.bfloat16)
    d_mixed_self = d_mixed_self.reshape(self_shape)
    dq_self, dk_self, dv_self = lax.map(
        self_back_one, (query_self, key_self, value_self, allowed_self, total_self, d_mixed_self)
    )
    dq_self = dq_self.reshape(tokens, head_width)
    dk_self = dk_self.reshape(tokens, head_width)
    dv_self = dv_self.reshape(tokens, head_width)
    grad_w_query = weight_grad(stream_full, dq_self)
    grad_w_pair = jnp.stack([weight_grad(context, dk_self), weight_grad(context, dv_self)])
    stream_term = back_project(dq_self, w_query)
    context_term = back_project(dk_self, w_pair[0]) + back_project(dv_self, w_pair[1])
    stream_summed, context_summed = back_self((stream_term, context_term))
    results = (
        result.astype(jnp.bfloat16),
        (d_attn + stream_summed).astype(jnp.bfloat16),
        context_summed.astype(jnp.bfloat16),
        source_summed.astype(jnp.bfloat16),
    )
    gradients = (
        grad_w_query,
        grad_w_pair,
        grad_w_out,
        grad_c_query,
        grad_c_pair,
        grad_c_out,
        grad_f_in,
        grad_f_out,
        jnp.stack([gain_first, gain_second, gain_third]),
        jnp.stack([bias_first, bias_second, bias_third]),
    )
    return (results, gradients)


def gather_shards(shards):
    return tuple(
        (
            lax.all_gather(shards[0], "dp", axis=0, tiled=True),
            lax.all_gather(shards[1], "dp", axis=1, tiled=True),
            lax.all_gather(shards[2], "dp", axis=1, tiled=True),
            lax.all_gather(shards[3], "dp", axis=0, tiled=True),
            lax.all_gather(shards[4], "dp", axis=1, tiled=True),
            lax.all_gather(shards[5], "dp", axis=1, tiled=True),
            lax.all_gather(shards[6], "dp", axis=0, tiled=True),
            lax.all_gather(shards[7], "dp", axis=0, tiled=True),
            lax.all_gather(shards[8], "dp", axis=1, tiled=True),
            lax.all_gather(shards[9], "dp", axis=1, tiled=True),
        )
    )


def scatter_shards(gradients):
    return tuple(
        (
            lax.psum_scatter(gradients[0], "dp", scatter_dimension=0, tiled=True),
            lax.psum_scatter(gradients[1], "dp", scatter_dimension=1, tiled=True),
            lax.psum_scatter(gradients[2], "dp", scatter_dimension=1, tiled=True),
            lax.psum_scatter(gradients[3], "dp", scatter_dimension=0, tiled=True),
            lax.psum_scatter(gradients[4], "dp", scatter_dimension=1, tiled=True),
            lax.psum_scatter(gradients[5], "dp", scatter_dimension=1, tiled=True),
            lax.psum_scatter(gradients[6], "dp", scatter_dimension=0, tiled=True),
            lax.psum_scatter(gradients[7], "dp", scatter_dimension=0, tiled=True),
            lax.psum_scatter(gradients[8], "dp", scatter_dimension=1, tiled=True),
            lax.psum_scatter(gradients[9], "dp", scatter_dimension=1, tiled=True),
        )
    )


def per_device(
    query_stream,
    context_stream,
    encoder_out,
    query_masks,
    source_segments,
    out_grad,
    self_query,
    self_key_value,
    self_output,
    cross_query,
    cross_key_value,
    cross_output,
    ffn_in,
    ffn_out,
    norm_gain,
    norm_bias,
):
    shards = (
        self_query,
        self_key_value,
        self_output,
        cross_query,
        cross_key_value,
        cross_output,
        ffn_in,
        ffn_out,
        norm_gain,
        norm_bias,
    )
    micro_count = query_stream.shape[0]
    groups = lax.axis_size("tensor")
    own_index = lax.axis_index("tensor")
    grad_scale = float(micro_count * query_stream.shape[1] * lax.axis_size("dp")) ** (-0.5)
    tokens = query_stream.shape[1]
    share = tokens // groups

    def mix_self(mixed, weight):

        def term(start, count):
            return jnp.dot(mixed, weight, preferred_element_type=jnp.float32)

        return lax.psum_scatter(
            term(jnp.int32(0), lax.axis_size("tensor") * (mixed.shape[0] // groups)).astype(
                jnp.bfloat16
            ),
            "tensor",
            scatter_dimension=0,
            tiled=True,
        ).astype(jnp.float32)

    def mix_cross(mixed, weight):

        def term(start, count):
            return jnp.dot(mixed, weight, preferred_element_type=jnp.float32)

        return lax.psum_scatter(
            term(jnp.int32(0), lax.axis_size("tensor") * (mixed.shape[0] // groups)).astype(
                jnp.bfloat16
            ),
            "tensor",
            scatter_dimension=0,
            tiled=True,
        ).astype(jnp.float32)

    def spread_first(value):
        return lax.all_gather(value, "tensor", axis=0, tiled=True)

    def spread_second(value):
        return lax.all_gather(value, "tensor", axis=0, tiled=True)

    def spread_third(value):
        return lax.all_gather(value, "tensor", axis=0, tiled=True)

    def back_cross(terms):
        return tuple(
            (
                lax.psum_scatter(
                    terms[0].astype(jnp.bfloat16), "tensor", scatter_dimension=0, tiled=True
                ).astype(jnp.float32),
                lax.psum_scatter(
                    terms[1].astype(jnp.bfloat16), "tensor", scatter_dimension=0, tiled=True
                ).astype(jnp.float32),
            )
        )

    def back_self(terms):
        return tuple(
            (
                lax.psum_scatter(
                    terms[0].astype(jnp.bfloat16), "tensor", scatter_dimension=0, tiled=True
                ).astype(jnp.float32),
                lax.psum_scatter(
                    terms[1].astype(jnp.bfloat16), "tensor", scatter_dimension=0, tiled=True
                ).astype(jnp.float32),
            )
        )

    reducers = (
        mix_self,
        spread_first,
        mix_cross,
        spread_second,
        back_cross,
        spread_third,
        back_self,
    )
    summed = None
    collected = []
    for micro_index in range(micro_count):
        weights = gather_shards(shards)
        stream_full = query_stream[micro_index]
        stream_part = lax.dynamic_slice_in_dim(stream_full, own_index * share, share, 0)
        results, gradients = micro_step(
            weights,
            stream_full,
            stream_part,
            context_stream[micro_index],
            encoder_out[micro_index],
            out_grad[micro_index],
            query_masks[micro_index],
            source_segments[micro_index],
            reducers,
        )
        collected.append(results)
        gradients = scatter_shards(gradients)
        summed = gradients if summed is None else jax.tree.map(jnp.add, summed, gradients)
    outputs = tuple((jnp.stack([item[member] for item in collected]) for member in range(4)))
    shared = (
        lax.psum(summed[6].astype(jnp.bfloat16), "tensor").astype(jnp.float32),
        lax.psum(summed[7].astype(jnp.bfloat16), "tensor").astype(jnp.float32),
        lax.psum(summed[8].astype(jnp.bfloat16), "tensor").astype(jnp.float32),
        lax.psum(summed[9].astype(jnp.bfloat16), "tensor").astype(jnp.float32),
    )
    summed = tuple(summed[:6]) + tuple(shared)
    summed = tuple((item * grad_scale for item in summed))
    return outputs + summed


def solution(mesh):
    in_specs = (
        P(None, "dp", None),
        P(None, "dp", None),
        P(None, "dp", None),
        P(None, "dp", None),
        P(None, "dp", None),
        P(None, ("dp", "tensor"), None),
        P("dp", "tensor"),
        P(None, "dp", "tensor"),
        P("tensor", "dp"),
        P("dp", "tensor"),
        P(None, "dp", "tensor"),
        P("tensor", "dp"),
        P("dp", None),
        P("dp", None),
        P(None, "dp"),
        P(None, "dp"),
    )
    out_specs = (
        P(None, ("dp", "tensor"), None),
        P(None, ("dp", "tensor"), None),
        P(None, ("dp", "tensor"), None),
        P(None, ("dp", "tensor"), None),
        P("dp", "tensor"),
        P(None, "dp", "tensor"),
        P("tensor", "dp"),
        P("dp", "tensor"),
        P(None, "dp", "tensor"),
        P("tensor", "dp"),
        P("dp", None),
        P("dp", None),
        P(None, "dp"),
        P(None, "dp"),
    )
    return jax.shard_map(
        per_device, mesh=mesh, in_specs=in_specs, out_specs=out_specs, check_vma=False
    )
```

profile of v0, /device:TPU:0, one launch (start us, length us, event | category | flops | bytes accessed | tf_op | source)
XLA Modules:
  0.0 1883.4 jit_solution(15373647643446173923)
XLA Ops:
  7.2 32.7 %all_gather.44 = bf16[2,512,128]{2,1,0:T(8,128)(2,1)S(1)} all-gather(bf16[2,64,128]{2,1,0:T(8,128)(2,1)} %param.39), channel_id=1, replica_groups=mesh['dp'=8,'tensor'=4] {'dp'}, dimensions={1}, use_global_device_ids=true | all-gather | bytes 294912 | tf_op jit(solution)/shard_map/all_gather | solution.py:284
  44.0 30.5 %all_gather.45 = bf16[512,128]{1,0:T(8,128)(2,1)S(1)} all-gather(bf16[64,128]{1,0:T(8,128)(2,1)S(1)} %copy-done.246), channel_id=1, replica_groups=mesh['dp'=8,'tensor'=4] {'dp'}, dimensions={0}, use_global_device_ids=true | all-gather | bytes 147456 | tf_op jit(solution)/shard_map/all_gather | solution.py:283
  80.1 30.5 %all_gather.46 = bf16[128,512]{0,1:T(8,128)(2,1)S(1)} all-gather(bf16[128,64]{0,1:T(8,128)(2,1)S(1)} %copy-done.247), channel_id=1, replica_groups=mesh['dp'=8,'tensor'=4] {'dp'}, dimensions={1}, use_global_device_ids=true | all-gather | bytes 147456 | tf_op jit(solution)/shard_map/all_gather | solution.py:285
  122.1 20.5 %all-gather.1 = bf16[8,64,3]{1,2,0:T(4,128)(2,1)S(1)} all-gather(bf16[1,64,3]{1,2,0:T(4,128)(2,1)S(1)} %bitcast.1499), channel_id=1, replica_groups=mesh['dp'=8,'tensor'=4] {'dp'}, dimensions={0}, use_global_device_ids=true | all-gather | bytes 3456 | tf_op jit(solution)/shard_map/all_gather | solution.py:292
  142.6 16.3 all-gather
  186.2 30.8 %all_gather.49 = bf16[2,512,128]{2,1,0:T(8,128)(2,1)S(1)} all-gather(bf16[2,64,128]{2,1,0:T(8,128)(2,1)S(1)} %copy-done.234), channel_id=1, replica_groups=mesh['dp'=8,'tensor'=4] {'dp'}, dimensions={1}, use_global_device_ids=true | all-gather | bytes 294912 | tf_op jit(solution)/shard_map/all_gather | solution.py:287
  219.8 30.6 %all_gather.51 = bf16[512,128]{1,0:T(8,128)(2,1)S(1)} all-gather(bf16[64,128]{1,0:T(8,128)(2,1)S(1)} %copy-done.248), channel_id=1, replica_groups=mesh['dp'=8,'tensor'=4] {'dp'}, dimensions={0}, use_global_device_ids=true | all-gather | bytes 147456 | tf_op jit(solution)/shard_map/all_gather | solution.py:286
  251.5 30.6 %all_gather.104 = bf16[128,512]{0,1:T(8,128)(2,1)S(1)} all-gather(bf16[128,64]{0,1:T(8,128)(2,1)S(1)} %copy-done.249), channel_id=1, replica_groups=mesh['dp'=8,'tensor'=4] {'dp'}, dimensions={1}, use_global_device_ids=true | all-gather | bytes 147456 | tf_op jit(solution)/shard_map/all_gather | solution.py:288
  305.2 17.8 reduce-scatter.43.cloned.1.call-done
  419.0 10.6 all-gather.19.cloned.1.call-done
  433.3 46.5 %all-gather.21.cloned.1.call-done = bf16[2048,512]{1,0:T(8,128)(2,1)} async-done(((bf16[256,512]{1,0:T(8,128)(2,1)}), bf16[2048,512]{1,0:T(8,128)(2,1)}) %all-gather.21.cloned.1.call-update) | async-done | bytes 2097168 | tf_op jit(solution)/shard_map/all_gather | solution.py:290
  483.9 21.8 %reduce-scatter.55.cloned.1.call-done = bf16[256,512]{1,0:T(8,128)(2,1)} async-done(((bf16[1024,512]{1,0:T(8,128)(2,1)}), bf16[256,512]{1,0:T(8,128)(2,1)}) %reduce-scatter.55.cloned.1.call-update) | async-done | bytes 262160 | tf_op jit(solution)/shard_map/reduce_scatter | solution.py:370
  505.7 27.4 %reduce-scatter.47.cloned.1.call-done = bf16[256,512]{1,0:T(8,128)(2,1)} async-done(((bf16[1024,512]{1,0:T(8,128)(2,1)}), bf16[256,512]{1,0:T(8,128)(2,1)}) %reduce-scatter.47.cloned.1.call-update) | async-done | bytes 262160 | tf_op jit(solution)/shard_map/reduce_scatter | solution.py:370
  533.2 27.5 %reduce-scatter.51.cloned.1.call-done = bf16[256,512]{1,0:T(8,128)(2,1)} async-done(((bf16[1024,512]{1,0:T(8,128)(2,1)}), bf16[256,512]{1,0:T(8,128)(2,1)}) %reduce-scatter.51.cloned.1.call-update) | async-done | bytes 262160 | tf_op jit(solution)/shard_map/reduce_scatter | solution.py:370
  600.2 15.1 all-gather.33.cloned.1.call-done
  684.7 12.6 reduce-scatter.61.cloned.1.call-done
  697.3 27.5 %reduce-scatter.69.cloned.1.call-done = bf16[256,512]{1,0:T(8,128)(2,1)} async-done(((bf16[1024,512]{1,0:T(8,128)(2,1)}), bf16[256,512]{1,0:T(8,128)(2,1)}) %reduce-scatter.69.cloned.1.call-update) | async-done | bytes 262160 | tf_op jit(solution)/shard_map/reduce_scatter | solution.py:391
  726.9 25.3 %reduce-scatter.65.cloned.1.call-done = bf16[256,512]{1,0:T(8,128)(2,1)} async-done(((bf16[1024,512]{1,0:T(8,128)(2,1)}), bf16[256,512]{1,0:T(8,128)(2,1)}) %reduce-scatter.65.cloned.1.call-update) | async-done | bytes 262160 | tf_op jit(solution)/shard_map/reduce_scatter | solution.py:391
  755.2 25.3 %reduce-scatter.57.cloned.1.call-done = bf16[256,512]{1,0:T(8,128)(2,1)} async-done(((bf16[1024,512]{1,0:T(8,128)(2,1)}), bf16[256,512]{1,0:T(8,128)(2,1)}) %reduce-scatter.57.cloned.1.call-update) | async-done | bytes 262160 | tf_op jit(solution)/shard_map/reduce_scatter | solution.py:391
  796.7 4.7 scatter_fusion.6
  826.5 4.7 scatter_fusion.4
  836.0 4.7 scatter_fusion.5
  846.3 4.8 scatter_fusion.2
  855.9 4.7 scatter_fusion.3
  866.5 4.7 scatter_fusion
  907.4 5.5 while.21
  919.6 5.9 while.20
  1003.0 11.2 reduce-scatter.87.cloned.1.call-done
  1014.2 27.5 %reduce-scatter.85.cloned.1.call-done = bf16[256,512]{1,0:T(8,128)(2,1)} async-done(((bf16[1024,512]{1,0:T(8,128)(2,1)}), bf16[256,512]{1,0:T(8,128)(2,1)}) %reduce-scatter.85.cloned.1.call-update) | async-done | bytes 262160 | tf_op jit(solution)/shard_map/reduce_scatter | solution.py:394
  1041.6 27.5 %reduce-scatter.83.cloned.1.call-done = bf16[256,512]{1,0:T(8,128)(2,1)} async-done(((bf16[1024,512]{1,0:T(8,128)(2,1)}), bf16[256,512]{1,0:T(8,128)(2,1)}) %reduce-scatter.83.cloned.1.call-update) | async-done | bytes 262160 | tf_op jit(solution)/shard_map/reduce_scatter | solution.py:394
  1069.1 27.6 %reduce-scatter.81.cloned.1.call-done = bf16[256,512]{1,0:T(8,128)(2,1)} async-done(((bf16[1024,512]{1,0:T(8,128)(2,1)}), bf16[256,512]{1,0:T(8,128)(2,1)}) %reduce-scatter.81.cloned.1.call-update) | async-done | bytes 262160 | tf_op jit(solution)/shard_map/reduce_scatter | solution.py:394
  1099.1 62.1 %reduce-scatter.101.cloned.1.call-done = f32[64,3]{1,0:T(8,128)} async-done(((f32[512,3]{1,0:T(8,128)}), f32[64,3]{1,0:T(8,128)}) %reduce-scatter.101.cloned.1.call-update) | async-done | bytes 784
  1162.0 62.8 %reduce-scatter.103.cloned.1.call-done = f32[64,3]{1,0:T(8,128)} async-done(((f32[512,3]{1,0:T(8,128)}), f32[64,3]{1,0:T(8,128)}) %reduce-scatter.103.cloned.1.call-update) | async-done | bytes 784
  1225.6 5.6 all-reduce.3
  1234.5 54.0 %reduce-scatter.97.cloned.1.call-done = f32[64,128]{1,0:T(8,128)} async-done(((f32[512,128]{1,0:T(8,128)}), f32[64,128]{1,0:T(8,128)}) %reduce-scatter.97.cloned.1.call-update) | async-done | bytes 32784
  1290.0 61.9 %reduce-scatter.89.cloned.1.call-done = f32[128,64]{0,1:T(8,128)} async-done(((f32[128,512]{0,1:T(8,128)}), f32[128,64]{0,1:T(8,128)}) %reduce-scatter.89.cloned.1.call-update) | async-done | bytes 32784 | tf_op jit(solution)/shard_map/reduce_scatter | solution.py:302
  1353.2 80.1 %all-reduce.8.cloned.1.call-done = (f32[2,512,128]{2,0,1:T(2,128)}, f32[2,512,128]{2,0,1:T(2,128)}) async-done(((f32[2,512,128]{2,0,1:T(2,128)}, f32[2,512,128]{2,0,1:T(2,128)}), (f32[2,512,128]{2,0,1:T(2,128)}, f32[2,512,128]{2,0,1:T(2,128)})) %all-reduce.8.cloned.1.call-update) | async-done | bytes 1048592
  1436.3 24.5 %reduce-scatter.71.cloned.1.call-done = bf16[256,512]{1,0:T(8,128)(2,1)} async-done(((bf16[1024,512]{1,0:T(8,128)(2,1)}), bf16[256,512]{1,0:T(8,128)(2,1)}) %reduce-scatter.71.cloned.1.call-update) | async-done | bytes 262160 | tf_op jit(solution)/shard_map/reduce_scatter | solution.py:403
  1461.9 26.9 %reduce-scatter.67.cloned.1.call-done = bf16[256,512]{1,0:T(8,128)(2,1)} async-done(((bf16[1024,512]{1,0:T(8,128)(2,1)}), bf16[256,512]{1,0:T(8,128)(2,1)}) %reduce-scatter.67.cloned.1.call-update) | async-done | bytes 262160 | tf_op jit(solution)/shard_map/reduce_scatter | solution.py:403
  1489.8 26.6 %reduce-scatter.63.cloned.1.call-done = bf16[256,512]{1,0:T(8,128)(2,1)} async-done(((bf16[1024,512]{1,0:T(8,128)(2,1)}), bf16[256,512]{1,0:T(8,128)(2,1)}) %reduce-scatter.63.cloned.1.call-update) | async-done | bytes 262160 | tf_op jit(solution)/shard_map/reduce_scatter | solution.py:403
  1517.4 26.4 %reduce-scatter.59.cloned.1.call-done = bf16[256,512]{1,0:T(8,128)(2,1)} async-done(((bf16[1024,512]{1,0:T(8,128)(2,1)}), bf16[256,512]{1,0:T(8,128)(2,1)}) %reduce-scatter.59.cloned.1.call-update) | async-done | bytes 262160 | tf_op jit(solution)/shard_map/reduce_scatter | solution.py:403
  1544.8 91.2 %reduce-scatter.93.cloned.1.call-done = f32[64,2048]{1,0:T(8,128)} async-done(((f32[512,2048]{1,0:T(8,128)}), f32[64,2048]{1,0:T(8,128)}) %reduce-scatter.93.cloned.1.call-update) | async-done | bytes 524304 | tf_op jit(solution)/shard_map/reduce_scatter | solution.py:306
  1637.7 89.4 %reduce-scatter.95.cloned.1.call-done = f32[256,512]{1,0:T(8,128)} async-done(((f32[2048,512]{1,0:T(8,128)}), f32[256,512]{1,0:T(8,128)}) %reduce-scatter.95.cloned.1.call-update) | async-done | bytes 524304 | tf_op jit(solution)/shard_map/reduce_scatter | solution.py:307
  1730.1 24.4 %reduce-scatter.79.cloned.1.call-done = bf16[256,512]{1,0:T(8,128)(2,1)} async-done(((bf16[1024,512]{1,0:T(8,128)(2,1)}), bf16[256,512]{1,0:T(8,128)(2,1)}) %reduce-scatter.79.cloned.1.call-update) | async-done | bytes 262160 | tf_op jit(solution)/shard_map/reduce_scatter | solution.py:406
  1754.5 27.3 %reduce-scatter.77.cloned.1.call-done = bf16[256,512]{1,0:T(8,128)(2,1)} async-done(((bf16[1024,512]{1,0:T(8,128)(2,1)}), bf16[256,512]{1,0:T(8,128)(2,1)}) %reduce-scatter.77.cloned.1.call-update) | async-done | bytes 262160 | tf_op jit(solution)/shard_map/reduce_scatter | solution.py:406
  1781.8 27.4 %reduce-scatter.75.cloned.1.call-done = bf16[256,512]{1,0:T(8,128)(2,1)} async-done(((bf16[1024,512]{1,0:T(8,128)(2,1)}), bf16[256,512]{1,0:T(8,128)(2,1)}) %reduce-scatter.75.cloned.1.call-update) | async-done | bytes 262160 | tf_op jit(solution)/shard_map/reduce_scatter | solution.py:406
  1809.3 27.3 %reduce-scatter.73.cloned.1.call-done = bf16[256,512]{1,0:T(8,128)(2,1)} async-done(((bf16[1024,512]{1,0:T(8,128)(2,1)}), bf16[256,512]{1,0:T(8,128)(2,1)}) %reduce-scatter.73.cloned.1.call-update) | async-done | bytes 262160 | tf_op jit(solution)/shard_map/reduce_scatter | solution.py:406
  1838.9 34.0 %all-reduce.10.cloned.1.call-done = (bf16[64,2048]{1,0:T(8,128)(2,1)}, bf16[256,512]{1,0:T(8,128)(2,1)}) async-done(((bf16[64,2048]{1,0:T(8,128)(2,1)}, bf16[256,512]{1,0:T(8,128)(2,1)}), (bf16[64,2048]{1,0:T(8,128)(2,1)}, bf16[256,512]{1,0:T(8,128)(2,1)})) %all-reduce.10.cloned.1.call-update) | async-done | bytes 524304 | tf_op jit(solution)/shard_map/psum | solution.py:443
  (1370 shorter events, 522.2 us)
Async XLA Ops:
  7.2 159.7 %reduce-scatter.41.cloned.1.call-start = ((), (), s32[]{:S(2)}) async-start(), calls=%async_computation.32 | async-start | bytes 1310720 | tf_op jit(solution)/shard_map/reduce_scatter | solution.py:356
  112.1 57.4 %reduce-scatter.53.cloned.1.call-start = ((), (), s32[]{:S(2)}) async-start(), calls=%async_computation.43 | async-start | bytes 1310720 | tf_op jit(solution)/shard_map/reduce_scatter | solution.py:356
  120.2 168.2 %all-gather.17.cloned.1.call-start = ((), (), s32[]{:S(2)}) async-start(), calls=%async_computation.33 | async-start | bytes 1310720 | tf_op jit(solution)/shard_map/all_gather | solution.py:380
  174.0 126.1 %reduce-scatter.45.cloned.1.call-start = ((), (), s32[]{:S(2)}) async-start(), calls=%async_computation.37 | async-start | bytes 1310720 | tf_op jit(solution)/shard_map/reduce_scatter | solution.py:356
  177.8 123.6 %reduce-scatter.49.cloned.1.call-start = ((), (), s32[]{:S(2)}) async-start(), calls=%async_computation.40 | async-start | bytes 1310720 | tf_op jit(solution)/shard_map/reduce_scatter | solution.py:356
  186.1 136.8 %reduce-scatter.43.cloned.1.call-start = ((), (), s32[]{:S(2)}) async-start(), calls=%async_computation.34 | async-start | bytes 1310720 | tf_op jit(solution)/shard_map/reduce_scatter | solution.py:370
  299.3 61.5 %all-gather.27.cloned.1.call-start = ((), (), s32[]{:S(2)}) async-start(), calls=%async_computation.44 | async-start | bytes 1310720 | tf_op jit(solution)/shard_map/all_gather | solution.py:380
  300.1 78.5 %all-gather.23.cloned.1.call-start = ((), (), s32[]{:S(2)}) async-start(), calls=%async_computation.38 | async-start | bytes 1310720 | tf_op jit(solution)/shard_map/all_gather | solution.py:380
  326.1 79.3 %all-gather.25.cloned.1.call-start = ((), (), s32[]{:S(2)}) async-start(), calls=%async_computation.41 | async-start | bytes 1310720 | tf_op jit(solution)/shard_map/all_gather | solution.py:380
  326.8 102.8 %all-gather.19.cloned.1.call-start = ((), (), s32[]{:S(2)}) async-start(), calls=%async_computation.35 | async-start | bytes 2359296 | tf_op jit(solution)/shard_map/all_gather | solution.py:289
  327.4 152.4 %all-gather.21.cloned.1.call-start = ((), (), s32[]{:S(2)}) async-start(), calls=%async_computation.36 | async-start | bytes 2359296 | tf_op jit(solution)/shard_map/all_gather | solution.py:290
  328.1 177.6 %reduce-scatter.55.cloned.1.call-start = ((), (), s32[]{:S(2)}) async-start(), calls=%async_computation.45 | async-start | bytes 1310720 | tf_op jit(solution)/shard_map/reduce_scatter | solution.py:370
  375.9 157.2 %reduce-scatter.47.cloned.1.call-start = ((), (), s32[]{:S(2)}) async-start(), calls=%async_computation.39 | async-start | bytes 1310720 | tf_op jit(solution)/shard_map/reduce_scatter | solution.py:370
  391.8 168.8 %reduce-scatter.51.cloned.1.call-start = ((), (), s32[]{:S(2)}) async-start(), calls=%async_computation.42 | async-start | bytes 1310720 | tf_op jit(solution)/shard_map/reduce_scatter | solution.py:370
  418.7 196.6 %all-gather.33.cloned.1.call-start = ((), (), s32[]{:S(2)}) async-start(), calls=%async_computation.50 | async-start | bytes 1310720 | tf_op jit(solution)/shard_map/all_gather | solution.py:383
  598.4 35.1 %all-gather.41.cloned.1.call-start = ((), (), s32[]{:S(2)}) async-start(), calls=%async_computation.58 | async-start | bytes 1310720 | tf_op jit(solution)/shard_map/all_gather | solution.py:383
  599.0 52.6 %all-gather.37.cloned.1.call-start = ((), (), s32[]{:S(2)}) async-start(), calls=%async_computation.54 | async-start | bytes 1310720 | tf_op jit(solution)/shard_map/all_gather | solution.py:383
  599.6 70.2 %all-gather.29.cloned.1.call-start = ((), (), s32[]{:S(2)}) async-start(), calls=%async_computation.46 | async-start | bytes 1310720 | tf_op jit(solution)/shard_map/all_gather | solution.py:383
  600.2 97.1 %reduce-scatter.61.cloned.1.call-start = ((), (), s32[]{:S(2)}) async-start(), calls=%async_computation.51 | async-start | bytes 1310720 | tf_op jit(solution)/shard_map/reduce_scatter | solution.py:391
  630.0 94.8 %reduce-scatter.69.cloned.1.call-start = ((), (), s32[]{:S(2)}) async-start(), calls=%async_computation.59 | async-start | bytes 1310720 | tf_op jit(solution)/shard_map/reduce_scatter | solution.py:391
  648.1 104.1 %reduce-scatter.65.cloned.1.call-start = ((), (), s32[]{:S(2)}) async-start(), calls=%async_computation.55 | async-start | bytes 1310720 | tf_op jit(solution)/shard_map/reduce_scatter | solution.py:391
  666.3 114.1 %reduce-scatter.57.cloned.1.call-start = ((), (), s32[]{:S(2)}) async-start(), calls=%async_computation.47 | async-start | bytes 1310720 | tf_op jit(solution)/shard_map/reduce_scatter | solution.py:391
  684.5 203.6 %all-gather.43.cloned.1.call-start = ((), (), s32[]{:S(2)}) async-start(), calls=%async_computation.60 | async-start | bytes 1310720 | tf_op jit(solution)/shard_map/all_gather | solution.py:386
  786.3 109.4 %all-gather.39.cloned.1.call-start = ((), (), s32[]{:S(2)}) async-start(), calls=%async_computation.56 | async-start | bytes 1310720 | tf_op jit(solution)/shard_map/all_gather | solution.py:386
  786.8 116.8 %all-gather.35.cloned.1.call-start = ((), (), s32[]{:S(2)}) async-start(), calls=%async_computation.52 | async-start | bytes 1310720 | tf_op jit(solution)/shard_map/all_gather | solution.py:386
  788.2 125.6 %all-gather.31.cloned.1.call-start = ((), (), s32[]{:S(2)}) async-start(), calls=%async_computation.48 | async-start | bytes 1310720 | tf_op jit(solution)/shard_map/all_gather | solution.py:386
  793.9 206.2 %reduce-scatter.99.cloned.1.call-start = ((), (), s32[]{:S(2)}) async-start(), calls=%async_computation.75 | async-start | bytes 294912
  815.4 186.2 %reduce-scatter.91.cloned.1.call-start = ((), (), s32[]{:S(2)}) async-start(), calls=%async_computation.71 | async-start | bytes 294912 | tf_op jit(solution)/shard_map/reduce_scatter | solution.py:305
  820.0 194.2 %reduce-scatter.87.cloned.1.call-start = ((), (), s32[]{:S(2)}) async-start(), calls=%async_computation.69 | async-start | bytes 1310720 | tf_op jit(solution)/shard_map/reduce_scatter | solution.py:394
  823.0 218.6 %reduce-scatter.85.cloned.1.call-start = ((), (), s32[]{:S(2)}) async-start(), calls=%async_computation.68 | async-start | bytes 1310720 | tf_op jit(solution)/shard_map/reduce_scatter | solution.py:394
  843.1 226.1 %reduce-scatter.83.cloned.1.call-start = ((), (), s32[]{:S(2)}) async-start(), calls=%async_computation.67 | async-start | bytes 1310720 | tf_op jit(solution)/shard_map/reduce_scatter | solution.py:394
  862.9 233.8 %reduce-scatter.81.cloned.1.call-start = ((), (), s32[]{:S(2)}) async-start(), calls=%async_computation.66 | async-start | bytes 1310720 | tf_op jit(solution)/shard_map/reduce_scatter | solution.py:394
  878.4 282.8 %reduce-scatter.101.cloned.1.call-start = ((), (), s32[]{:S(2)}) async-start(), calls=%async_computation.76 | async-start | bytes 294912
  886.8 338.0 %reduce-scatter.103.cloned.1.call-start = ((), (), s32[]{:S(2)}) async-start(), calls=%async_computation.77 | async-start | bytes 294912
  887.9 400.6 %reduce-scatter.97.cloned.1.call-start = ((), (), s32[]{:S(2)}) async-start(), calls=%async_computation.74 | async-start | bytes 294912
  948.7 403.2 %reduce-scatter.89.cloned.1.call-start = ((), (), s32[]{:S(2)}) async-start(), calls=%async_computation.70 | async-start | bytes 294912 | tf_op jit(solution)/shard_map/reduce_scatter | solution.py:302
  953.2 480.1 %all-reduce.8.cloned.1.call-start = ((), (), s32[]{:S(2)}) async-start(), calls=%async_computation.78 | async-start | bytes 2097152
  961.6 499.3 %reduce-scatter.71.cloned.1.call-start = ((), (), s32[]{:S(2)}) async-start(), calls=%async_computation.61 | async-start | bytes 1310720 | tf_op jit(solution)/shard_map/reduce_scatter | solution.py:403
  963.1 525.6 %reduce-scatter.67.cloned.1.call-start = ((), (), s32[]{:S(2)}) async-start(), calls=%async_computation.57 | async-start | bytes 1310720 | tf_op jit(solution)/shard_map/reduce_scatter | solution.py:403
  964.7 551.7 %reduce-scatter.63.cloned.1.call-start = ((), (), s32[]{:S(2)}) async-start(), calls=%async_computation.53 | async-start | bytes 1310720 | tf_op jit(solution)/shard_map/reduce_scatter | solution.py:403
  966.2 577.6 %reduce-scatter.59.cloned.1.call-start = ((), (), s32[]{:S(2)}) async-start(), calls=%async_computation.49 | async-start | bytes 1310720 | tf_op jit(solution)/shard_map/reduce_scatter | solution.py:403
  967.8 668.2 %reduce-scatter.93.cloned.1.call-start = ((), (), s32[]{:S(2)}) async-start(), calls=%async_computation.72 | async-start | bytes 4718592 | tf_op jit(solution)/shard_map/reduce_scatter | solution.py:306
  976.1 751.1 %reduce-scatter.95.cloned.1.call-start = ((), (), s32[]{:S(2)}) async-start(), calls=%async_computation.73 | async-start | bytes 4718592 | tf_op jit(solution)/shard_map/reduce_scatter | solution.py:307
  988.7 765.8 %reduce-scatter.79.cloned.1.call-start = ((), (), s32[]{:S(2)}) async-start(), calls=%async_computation.65 | async-start | bytes 1310720 | tf_op jit(solution)/shard_map/reduce_scatter | solution.py:406
  991.6 790.2 %reduce-scatter.77.cloned.1.call-start = ((), (), s32[]{:S(2)}) async-start(), calls=%async_computation.64 | async-start | bytes 1310720 | tf_op jit(solution)/shard_map/reduce_scatter | solution.py:406
  994.0 815.2 %reduce-scatter.75.cloned.1.call-start = ((), (), s32[]{:S(2)}) async-start(), calls=%async_computation.63 | async-start | bytes 1310720 | tf_op jit(solution)/shard_map/reduce_scatter | solution.py:406
  996.5 840.1 %reduce-scatter.73.cloned.1.call-start = ((), (), s32[]{:S(2)}) async-start(), calls=%async_computation.62 | async-start | bytes 1310720 | tf_op jit(solution)/shard_map/reduce_scatter | solution.py:406
  1233.3 639.6 %all-reduce.10.cloned.1.call-start = ((), (), s32[]{:S(2)}) async-start(), calls=%async_computation.79 | async-start | bytes 1048576 | tf_op jit(solution)/shard_map/psum | solution.py:443
  (306 other events, 5634.9 us)
Sparse Core Ops, SparseCore 0:
  112.2 25.8 reduce-scatter.40
  140.8 24.8 reduce-scatter.52
  174.2 15.4 all-gather.16
  192.1 24.9 reduce-scatter.44
  219.6 24.8 reduce-scatter.48
  299.4 23.4 reduce-scatter.42
  324.5 16.7 all-gather.26
  342.9 16.7 all-gather.22
  361.3 16.7 all-gather.24
  380.3 49.2 all-gather.18
  432.0 47.7 all-gather.20
  482.3 23.3 reduce-scatter.54
  508.2 24.8 reduce-scatter.46
  535.7 24.8 reduce-scatter.50
  598.5 16.7 all-gather.32
  616.7 16.7 all-gather.40
  634.9 16.7 all-gather.36
  653.1 16.7 all-gather.28
  672.3 24.9 reduce-scatter.60
  699.8 24.8 reduce-scatter.68
  727.3 24.9 reduce-scatter.64
  755.5 24.8 reduce-scatter.56
  786.4 16.7 all-gather.42
  805.1 16.7 all-gather.38
  823.5 16.7 all-gather.34
  842.2 16.7 all-gather.30
  862.1 61.2 reduce-scatter.98
  926.8 60.2 reduce-scatter.90
  990.2 23.8 reduce-scatter.86
  1016.7 24.8 reduce-scatter.84
  1044.2 24.8 reduce-scatter.82
  1071.8 24.8 reduce-scatter.80
  1099.9 61.2 reduce-scatter.100
  1164.5 60.2 reduce-scatter.102
  1228.1 60.2 reduce-scatter.96
  1291.6 60.2 reduce-scatter.88
  1355.8 77.4 all-reduce.7
  1436.6 24.2 reduce-scatter.70
  1463.8 24.8 reduce-scatter.66
  1491.4 24.8 reduce-scatter.62
  1518.9 24.8 reduce-scatter.58
  1547.9 88.0 reduce-scatter.92
  1639.4 87.6 reduce-scatter.94
  1729.9 24.6 reduce-scatter.78
  1756.9 24.8 reduce-scatter.76
  1784.4 24.8 reduce-scatter.74
  1811.7 24.8 reduce-scatter.72
  1839.6 33.2 all-reduce.9
where the time goes:
time: 1900 us; the launch traced here: 1880 us
  waiting for transfers between devices  1110 us (58%)
  matrix products  232 us (12%)
  blocking collectives  228 us (12%)
  local copies, waits for them, and re-layouts  165 us (9%)
  other arithmetic  118 us (6%)
  between operations  21.2 us (1%)
    unnamed x53, waiting for transfers between devices  264 us
    reduce_scatter x4, waiting for transfers between devices, back_self(): lax.psum_scatter(terms[1].astype(jnp.bfloat16), 'tensor', scatter_dimensi...  106 us
    reduce_scatter x4, waiting for transfers between devices, back_self(): lax.psum_scatter(terms[0].astype(jnp.bfloat16), 'tensor', scatter_dimensi...  104 us
    reduce_scatter x4, waiting for transfers between devices, mix_cross(): lax.psum_scatter(term(jnp.int32(0), lax.axis_size('tensor') * (mixed.shap...  94.5 us
    reduce_scatter x4, waiting for transfers between devices, back_cross(): lax.psum_scatter(terms[1].astype(jnp.bfloat16), 'tensor', scatter_dimensi...  93.7 us
    reduce_scatter x1, waiting for transfers between devices, scatter_shards(): lax.psum_scatter(gradients[6], 'dp', scatter_dimension=0, tiled=True)  91.2 us
    reduce_scatter x4, waiting for transfers between devices, back_cross(): lax.psum_scatter(terms[0].astype(jnp.bfloat16), 'tensor', scatter_dimensi...  90.7 us
    reduce_scatter x1, waiting for transfers between devices, scatter_shards(): lax.psum_scatter(gradients[7], 'dp', scatter_dimension=0, tiled=True)  89.4 us
  transfers between devices with their start and end apart: 48, of which 34 were waited for; matrix products, arithmetic and copies ran while one was open for 23% of the time, Pallas kernels for 0%

commit v1 on v0

v1 whole, which is shorter than its diff:
```python
import functools

import jax
import jax.numpy as jnp
from jax import lax
from jax.experimental import pallas as pl
from jax.experimental.pallas import tpu as pltpu
from jax.sharding import PartitionSpec as P

HEAD_DIM = 64
SLOT = 64
SEG_MOST = 128
QUAD = 4 * HEAD_DIM
PAIR = 2 * HEAD_DIM
NZ, NX, NY, NC = 4, 2, 2, 2
SELF, CROSS, UP, DOWN = 0, 4, 8, 12
BF16 = jnp.bfloat16
F32 = jnp.float32
MESH = pl.DeviceIdType.MESH

epsilon = 1e-05
neg_fill = -1e30
gelu_coef = 0.7978845608028654
gelu_cube = 0.044715
VMEM_LIMIT = 65400 * 1024


def mm(left, right):
    return jnp.dot(left, right, preferred_element_type=F32)


def mm_nt(left, right):
    return lax.dot_general(left, right, (((1,), (1,)), ((), ())), preferred_element_type=F32)


def mm_tn(left, right):
    return lax.dot_general(left, right, (((0,), (0,)), ((), ())), preferred_element_type=F32)


def norm_forward(value, gain, bias):
    center = jnp.mean(value, axis=-1, keepdims=True)
    shifted = value - center
    factor = lax.rsqrt(jnp.mean(shifted * shifted, axis=-1, keepdims=True) + epsilon)
    normed = shifted * factor
    return normed * gain + bias, normed, factor


def norm_backward(incoming, normed, factor, gain):
    scaled = incoming * gain
    inside = (
        scaled
        - jnp.mean(scaled, axis=-1, keepdims=True)
        - normed * jnp.mean(scaled * normed, axis=-1, keepdims=True)
    )
    return (
        factor * inside,
        jnp.sum(incoming * normed, axis=0, keepdims=True),
        jnp.sum(incoming, axis=0, keepdims=True),
    )


def columns(r, kind):
    parts = [r.w[kind, t // NC, t % NC].reshape(-1, 128) for t in range(NY * NC)]
    return jnp.concatenate(parts, axis=1)


def ffn_columns(r, j):
    parts = [r.w[UP + k, j // NC, j % NC].reshape(-1, 128) for k in range(4)]
    return jnp.concatenate(parts, axis=1)


def ffn_rows(r, j):
    parts = []
    for t in range(NY * NC):
        rows = [r.w[DOWN + k, t // NC, t % NC, j, b] for b in range(NX) for k in range(4)]
        parts.append(jnp.concatenate(rows, axis=0))
    return jnp.concatenate(parts, axis=1)


def grad_place(r, kind):
    if kind >= UP:
        return r.g_ffn, kind - UP
    return r.w, kind + UP


def store_columns(r, value, kind):
    ref, at = grad_place(r, kind)
    for t in range(NY * NC):
        ref[at, t // NC, t % NC] = value[:, t * 128 : (t + 1) * 128].reshape(NZ, NX, -1, 128)


def head_marks():
    lane = lax.broadcasted_iota(jnp.int32, (1, QUAD), 1) // HEAD_DIM
    return [jnp.where(lane == h, 1.0, 0.0).astype(BF16) for h in range(4)]


def spread_heads(rows, marks):
    return jnp.concatenate([rows * mark for mark in marks], axis=0)


def fold_pairs(weights, rows):
    first = lax.broadcasted_iota(jnp.int32, (SLOT, PAIR), 1) < HEAD_DIM
    parts = []
    for p in range(2):
        cut = slice(p * PAIR, (p + 1) * PAIR)
        full = mm_tn(weights[:, cut], rows[:, cut])
        parts.append(jnp.where(first, full[:SLOT], full[SLOT:]))
    return jnp.concatenate(parts, axis=1)


def soft_keys(scores, allowed):
    scores = jnp.where(allowed, scores, neg_fill)
    top = jnp.max(scores, axis=0, keepdims=True)
    raised = jnp.exp(scores - top)
    return (raised * (1.0 / jnp.sum(raised, axis=0, keepdims=True))).astype(BF16)


def attend_back(probs, keys, values, queries, d_mixed, marks):
    d_spread = spread_heads(d_mixed, marks)
    d_probs = mm_nt(values, d_spread)
    wide = probs.astype(F32)
    inner = jnp.sum(wide * d_probs, axis=0, keepdims=True)
    d_scores = (wide * (d_probs - inner)).astype(BF16)
    d_values = mm(probs, d_spread).astype(BF16)
    d_keys = mm(d_scores, spread_heads(queries, marks)).astype(BF16)
    d_queries = (fold_pairs(d_scores, keys) * HEAD_DIM ** (-0.5)).astype(BF16)
    return d_queries, d_keys, d_values


class Refs:
    pass


def frame_rows(share):
    return (share // SLOT) * SEG_MOST + 16


def window_rows():
    return SEG_MOST + 16


def window_table(starts, share, enc_len):
    frame, wide = frame_rows(share), window_rows()
    base = jnp.minimum(starts[:, :1] // 16 * 16, enc_len - frame)
    begin = starts[:, :-1] - base
    at = jnp.minimum(begin // 16 * 16, frame - wide)
    low = begin - at
    high = low + starts[:, 1:] - starts[:, :-1]
    return jnp.concatenate(
        [base // 16, (enc_len - frame - base) // 16, at // 16, low, high, (frame - wide - at) // 16],
        axis=1,
    )


def frame_start(r, m):
    return r.table[m, 0] * 16


def slot_window(r, m, s):
    at = r.table[m, 2 + s] * 16
    return at, r.table[m, 2 + r.slots + s], r.table[m, 2 + 2 * r.slots + s]


def slot_shift(r, m, s):
    return r.table[m, 2 + 3 * r.slots + s] * 16


def forward_self(r, m):
    marks = head_marks()
    stream, context = r.stream[m], r.context[m]
    queries = (mm(stream, columns(r, SELF + 0)) * HEAD_DIM ** (-0.5)).astype(BF16)
    keys = mm(context, columns(r, SELF + 1)).astype(BF16)
    values = mm(context, columns(r, SELF + 2)).astype(BF16)
    r.q_self[m], r.k_self[m], r.v_self[m] = queries, keys, values
    row = lax.broadcasted_iota(jnp.int32, (SLOT, QUAD), 0)
    lane = lax.broadcasted_iota(jnp.int32, (SLOT, QUAD), 1) % SLOT
    place = jnp.where(lane == 2 * (row % 32) + row // 32, 1.0, 0.0).astype(BF16)
    mixed = []
    for s in range(r.slots):
        rows = slice(s * SLOT, (s + 1) * SLOT)
        bits = r.masks[m, s * 32 : (s + 1) * 32].astype(F32)
        bits = jnp.concatenate([bits[:, :SLOT], bits[:, SLOT:]], axis=0).astype(BF16)
        allowed = mm_tn(bits, place) > 0.5
        halves = []
        for g in range(r.quads):
            cut = slice(g * QUAD, (g + 1) * QUAD)
            scores = mm_nt(keys[rows, cut], spread_heads(queries[rows, cut], marks))
            probs = soft_keys(scores, allowed)
            r.p_self[m, s, g] = probs
            halves.append(fold_pairs(probs, values[rows, cut]).astype(BF16))
        mixed.append(jnp.concatenate(halves, axis=1))
    mixed = jnp.concatenate(mixed, axis=0)
    r.mixed_self[m] = mixed
    attn = mm_nt(mixed, columns(r, SELF + 3))
    first, normed, factor = norm_forward(
        stream.astype(F32) + attn, r.norms[0:1, :], r.norms[3:4, :]
    )
    r.residual[m], r.factor[m, :, 0:1] = first, factor
    r.normed1[m] = normed.astype(BF16)
    r.first_low[m] = first.astype(BF16)


def forward_cross(r, m):
    marks = head_marks()
    base = frame_start(r, m)
    source = r.big1[m, pl.ds(base, r.frame), :]
    r.source[m] = source
    r.k_cross[m] = mm(source, columns(r, CROSS + 1)).astype(BF16)
    r.v_cross[m] = mm(source, columns(r, CROSS + 2)).astype(BF16)
    queries = (mm(r.first_low[m], columns(r, CROSS + 0)) * HEAD_DIM ** (-0.5)).astype(BF16)
    r.q_cross[m] = queries
    wide = window_rows()
    row = lax.broadcasted_iota(jnp.int32, (wide, QUAD), 0)
    mixed = []
    for s in range(r.slots):
        rows = slice(s * SLOT, (s + 1) * SLOT)
        at, low, high = slot_window(r, m, s)
        allowed = (row >= low) & (row < high)
        halves = []
        for g in range(r.quads):
            cut = slice(g * QUAD, (g + 1) * QUAD)
            keys = r.k_cross[m, pl.ds(at, wide), cut]
            values = r.v_cross[m, pl.ds(at, wide), cut]
            scores = mm_nt(keys, spread_heads(queries[rows, cut], marks))
            probs = soft_keys(scores, allowed)
            r.p_cross[m, s, g] = probs
            halves.append(fold_pairs(probs, values).astype(BF16))
        mixed.append(jnp.concatenate(halves, axis=1))
    mixed = jnp.concatenate(mixed, axis=0)
    r.mixed_cross[m] = mixed
    attn = mm_nt(mixed, columns(r, CROSS + 3))
    second, normed, factor = norm_forward(
        r.residual[m] + attn, r.norms[1:2, :], r.norms[4:5, :]
    )
    r.residual[m], r.factor[m, :, 1:2] = second, factor
    r.normed2[m] = normed.astype(BF16)
    r.second_low[m] = second.astype(BF16)


def feed_forward(r, m):
    second = r.residual[m]
    low = r.second_low[m]
    rows = pl.ds(pl.multiple_of(m * r.share, r.share), r.share)
    total = second
    for j in range(4):
        inner = mm(low, ffn_columns(r, j))
        square = inner * inner
        bent = jnp.tanh(gelu_coef * inner * (1.0 + gelu_cube * square))
        half = 0.5 * (1.0 + bent)
        hidden = (inner * half).astype(BF16)
        r.big1[j, rows, :] = hidden
        slope = half + 0.5 * inner * (1.0 - bent * bent) * gelu_coef * (
            1.0 + 3.0 * gelu_cube * square
        )
        r.shifted[j * r.share : (j + 1) * r.share, :] = slope.astype(BF16)
        total = total + mm(hidden, ffn_rows(r, j))
    result, normed, factor = norm_forward(total, r.norms[2:3, :], r.norms[5:6, :])
    r.d_first[m] = result.astype(BF16)
    d_third, gain, bias = norm_backward(
        r.cotangent[m].astype(F32), normed, factor, r.norms[2:3, :]
    )
    r.sums[2:3, :] += gain
    r.sums[5:6, :] += bias
    d_low = d_third.astype(BF16)
    r.d_third[m] = d_low
    d_second = d_third
    for j in range(4):
        slope = r.shifted[j * r.share : (j + 1) * r.share, :].astype(F32)
        d_inner = (mm_nt(d_low, ffn_rows(r, j)) * slope).astype(BF16)
        r.big2[j, rows, :] = d_inner
        d_second = d_second + mm_nt(d_inner, ffn_columns(r, j))
    d_cross, gain, bias = norm_backward(d_second, r.normed2[m].astype(F32), r.factor[m, :, 1:2], r.norms[1:2, :])
    r.sums[1:2, :] += gain
    r.sums[4:5, :] += bias
    r.residual[m] = d_cross
    r.d_second[m] = d_cross.astype(BF16)


def tokens(ref):
    value = ref[...]
    return value.reshape(-1, value.shape[-1])


def ffn_grads(r, j):
    up = mm_tn(tokens(r.second_low), r.big2[j]).astype(BF16)
    for k in range(4):
        r.g_ffn[k, j // NC, j % NC] = up[:, k * 128 : (k + 1) * 128].reshape(NZ, NX, -1, 128)
    down = mm_tn(tokens(r.d_third), r.big1[j]).astype(BF16)
    for t in range(NY * NC):
        for i in range(2):
            for b in range(NX):
                for n in range(2):
                    r.g_ffn[4 + 2 * i + n, t // NC, t % NC, j, b] = down[
                        t * 128 + i * 64 : t * 128 + (i + 1) * 64,
                        b * 256 + n * 128 : b * 256 + (n + 1) * 128,
                    ]


def clear_pads(r):
    for s in range(r.slots):
        r.big2[s] = jnp.zeros(r.big2.shape[1:], BF16)
    r.shifted[...] = jnp.zeros(r.shifted.shape, BF16)


def backward_cross(r, m):
    marks = head_marks()
    wide = window_rows()
    reach = r.frame - wide
    d_mixed = mm(r.d_second[m], columns(r, CROSS + 3)).astype(BF16)
    queries = r.q_cross[m]
    d_queries = []
    windows = [slot_window(r, m, s) for s in range(r.slots)]
    for g in range(r.quads):
        cut = slice(g * QUAD, (g + 1) * QUAD)
        column = []
        for s in range(r.slots):
            rows = slice(s * SLOT, (s + 1) * SLOT)
            at = windows[s][0]
            d_q, d_k, d_v = attend_back(
                r.p_cross[m, s, g],
                r.k_cross[m, pl.ds(at, wide), cut],
                r.v_cross[m, pl.ds(at, wide), cut],
                queries[rows, cut],
                d_mixed[rows, cut],
                marks,
            )
            r.big2[s, reach : reach + wide, :QUAD] = d_k
            r.big2[s, reach : reach + wide, QUAD:] = d_v
            column.append(d_q)
        d_queries.append(jnp.concatenate(column, axis=0))
        total = None
        for s in range(r.slots):
            piece = r.big2[s, pl.ds(slot_shift(r, m, s), r.frame), :]
            total = piece if total is None else total + piece
        r.k_cross[m, :, cut] = total[:, :QUAD]
        r.v_cross[m, :, cut] = total[:, QUAD:]
    d_queries = jnp.concatenate(d_queries, axis=1)
    r.q_cross[m] = d_queries
    d_first = r.residual[m] + mm_nt(d_queries, columns(r, CROSS + 0))
    d_attn, gain, bias = norm_backward(d_first, r.normed1[m].astype(F32), r.factor[m, :, 0:1], r.norms[0:1, :])
    r.sums[0:1, :] += gain
    r.sums[3:4, :] += bias
    r.residual[m] = d_attn
    r.d_first[m] = d_attn.astype(BF16)
    source_term = mm_nt(r.k_cross[m], columns(r, CROSS + 1)) + mm_nt(
        r.v_cross[m], columns(r, CROSS + 2)
    )
    edge = r.enc_len - r.frame
    r.shifted[edge : edge + r.frame, :] = source_term.astype(BF16)
    r.big1[m] = r.shifted[pl.ds(r.table[m, 1] * 16, r.enc_len), :]


def cross_grads(r):
    store_columns(r, mm_tn(tokens(r.first_low), tokens(r.q_cross)).astype(BF16), CROSS)
    store_columns(r, mm_tn(tokens(r.source), tokens(r.k_cross)).astype(BF16), CROSS + 1)
    store_columns(r, mm_tn(tokens(r.source), tokens(r.v_cross)).astype(BF16), CROSS + 2)
    store_columns(r, mm_tn(tokens(r.d_second), tokens(r.mixed_cross)).astype(BF16), CROSS + 3)


def backward_self(r, m):
    marks = head_marks()
    d_mixed = mm(r.d_first[m], columns(r, SELF + 3)).astype(BF16)
    queries, keys, values = r.q_self[m], r.k_self[m], r.v_self[m]
    out = []
    for s in range(r.slots):
        rows = slice(s * SLOT, (s + 1) * SLOT)
        halves = []
        for g in range(r.quads):
            cut = slice(g * QUAD, (g + 1) * QUAD)
            halves.append(
                attend_back(
                    r.p_self[m, s, g],
                    keys[rows, cut],
                    values[rows, cut],
                    queries[rows, cut],
                    d_mixed[rows, cut],
                    marks,
                )
            )
        out.append([jnp.concatenate([half[i] for half in halves], axis=1) for i in range(3)])
    d_q, d_k, d_v = [jnp.concatenate([item[i] for item in out], axis=0) for i in range(3)]
    r.q_self[m], r.k_self[m], r.v_self[m] = d_q, d_k, d_v
    r.cotangent[m] = (r.residual[m] + mm_nt(d_q, columns(r, SELF + 0))).astype(BF16)
    r.second_low[m] = (
        mm_nt(d_k, columns(r, SELF + 1)) + mm_nt(d_v, columns(r, SELF + 2))
    ).astype(BF16)


def self_grads(r):
    store_columns(r, mm_tn(tokens(r.stream), tokens(r.q_self)).astype(BF16), SELF)
    store_columns(r, mm_tn(tokens(r.context), tokens(r.k_self)).astype(BF16), SELF + 1)
    store_columns(r, mm_tn(tokens(r.context), tokens(r.v_self)).astype(BF16), SELF + 2)


def output_grads(r):
    store_columns(r, mm_tn(tokens(r.d_first), tokens(r.mixed_self)).astype(BF16), SELF + 3)


class Place:
    def __init__(self, groups):
        d, t = lax.axis_index("dp"), lax.axis_index("tensor")
        high, self.low = lax.div(d, groups), lax.rem(d, groups)
        self.groups = groups
        self.a, self.b = lax.div(high, NX), lax.rem(high, NX)
        self.y, self.c = lax.div(t, NC), lax.rem(t, NC)
        self.t = t

    def device(self, a=None, b=None, y=None, c=None):
        a, b = self.a if a is None else a, self.b if b is None else b
        y, c = self.y if y is None else y, self.c if c is None else c
        return ((a * NX + b) * self.groups + self.low, y * NC + c)

    def up(self, k):
        return lax.rem(self.a + k, NZ)

    def peer(self, axis, k=0):
        if axis == "z":
            return self.device(a=self.up(k))
        if axis == "x":
            return self.device(b=1 - self.b)
        if axis == "y":
            return self.device(y=1 - self.y)
        if axis == "core":
            return self.device(c=1 - self.c)
        return self.device(y=1 - self.y, c=1 - self.c)


class Link:
    def __init__(self, r):
        self.r = r
        self.used = 0
        self.all = []

    def slot(self):
        self.used += 1
        return self.used - 1

    def send(self, key, source, target, device):
        return pltpu.make_async_remote_copy(
            src_ref=source,
            dst_ref=target,
            send_sem=self.r.send_sems.at[key],
            recv_sem=self.r.recv_sems.at[key],
            device_id=device,
            device_id_type=MESH,
        )


class Stages:
    def __init__(self, link, counts):
        self.link = link
        self.keys = [[link.slot() for _ in range(n)] for n in counts]
        link.all.append(self)

    def start(self, stage):
        for copy in self.copies(stage):
            copy.start()

    def wait(self, stage):
        for copy in self.copies(stage):
            copy.wait_recv()

    def drain(self):
        for stage in range(len(self.keys)):
            for copy in self.copies(stage):
                copy.wait_send()


class Gather(Stages):
    def __init__(self, link, place, first, count, order):
        super().__init__(link, (NZ - 1, 1, 1, 1))
        self.p, self.kinds, self.order = place, pl.ds(first, count), order

    def copies(self, stage):
        p, w, send = self.p, self.link.r.w, self.link.send
        keys = self.keys[stage]
        if stage == 0:
            ref = w.at[self.kinds, p.y, p.c, p.a, p.b]
            return [send(keys[k - 1], ref, ref, p.peer("z", k)) for k in range(1, NZ)]
        if stage == 1:
            ref = w.at[self.kinds, p.y, p.c, :, p.b]
            return [send(keys[0], ref, ref, p.peer(self.order[0]))]
        if stage == 2:
            if self.order == "xy":
                ref = w.at[self.kinds, p.y, p.c]
            else:
                ref = w.at[self.kinds, :, p.c, :, p.b]
            return [send(keys[0], ref, ref, p.peer(self.order[1]))]
        ref = w.at[self.kinds, :, p.c]
        return [send(keys[0], ref, ref, p.peer("core"))]


class GatherNorms(Stages):
    def __init__(self, link, place):
        super().__init__(link, (NZ - 1, 1))
        self.p = place

    def copies(self, stage):
        p, pack, send = self.p, self.link.r.pack, self.link.send
        keys = self.keys[stage]
        if stage == 0:
            ref = pack.at[p.a, p.b]
            return [send(keys[k - 1], ref, ref, p.peer("z", k)) for k in range(1, NZ)]
        ref = pack.at[:, p.b]
        return [send(keys[0], ref, ref, p.peer("x"))]


class Scatter(Stages):
    def __init__(self, link, place, first, count, order, boxes):
        super().__init__(link, (1, 1, 1, NZ - 1))
        self.p, self.count, self.order, self.boxes = place, count, order, boxes
        self.ref, at = grad_place(link.r, first)
        self.first = at
        self.kinds = pl.ds(at, count)

    def parts(self, stage):
        p = self.p
        every = slice(None)
        if stage == 0:
            return (every, 1 - p.c), (every, p.c)
        if stage == 1:
            if self.order == "xy":
                return (every, p.c, every, 1 - p.b), (every, p.c, every, p.b)
            return (1 - p.y, p.c), (p.y, p.c)
        if self.order == "xy":
            return (1 - p.y, p.c, every, p.b), (p.y, p.c, every, p.b)
        return (p.y, p.c, every, 1 - p.b), (p.y, p.c, every, p.b)

    def copies(self, stage):
        p, send, keys = self.p, self.link.send, self.keys[stage]
        if stage < 3:
            axis = "core" if stage == 0 else self.order[stage - 1]
            source = self.ref.at[(self.kinds, *self.parts(stage)[0])]
            return [send(keys[0], source, self.boxes[stage], p.peer(axis))]
        return [
            send(
                keys[k - 1],
                self.ref.at[self.kinds, p.y, p.c, p.up(k), p.b],
                self.boxes[3].at[k - 1],
                p.peer("z", k),
            )
            for k in range(1, NZ)
        ]

    def add(self, stage):
        self.wait(stage)
        keep = self.parts(stage)[1]
        for k in range(self.count):
            at = (self.first + k, *keep)
            self.ref[at] = self.ref[at] + self.boxes[stage][k]

    def step(self, stage):
        self.add(stage)
        self.start(stage + 1)

    def total(self, k):
        p = self.p
        own = self.ref[self.first + k, p.y, p.c, p.a, p.b].astype(F32)
        box = self.boxes[3]
        return own + box[0, k].astype(F32) + box[1, k].astype(F32) + box[2, k].astype(F32)


def scatter_boxes(name, count, order):
    second = (NY, NZ) if order == "xy" else (NZ, NX)
    tile = (64, 128)
    return [
        (name + "0", pltpu.VMEM((count, NY, NZ, NX, *tile), BF16)),
        (name + "1", pltpu.VMEM((count, *second, *tile), BF16)),
        (name + "2", pltpu.VMEM((count, NZ, *tile), BF16)),
        (name + "3", pltpu.VMEM((NZ - 1, count, *tile), BF16)),
    ]


SCATTERS = {
    "up": (UP, 4, "xy"),
    "down": (DOWN, 4, "xy"),
    "cross": (CROSS, 4, "xy"),
    "mix": (SELF + 3, 1, "xy"),
    "query": (SELF, 1, "xy"),
    "pair": (SELF + 1, 2, "yx"),
}


class ScatterNorms(Stages):
    def __init__(self, link, place):
        super().__init__(link, (1, 1, 1, NZ - 1))
        self.p = place

    def copies(self, stage):
        p, r, send, keys = self.p, self.link.r, self.link.send, self.keys[stage]
        if stage == 0:
            return [send(keys[0], r.g_norm, r.n_box0, p.peer("core"))]
        if stage == 1:
            return [send(keys[0], r.n_sum, r.n_box1, p.peer("y"))]
        if stage == 2:
            return [send(keys[0], r.n_all.at[:, 1 - p.b], r.n_box2, p.peer("x"))]
        return [
            send(keys[k - 1], r.n_half.at[p.up(k)], r.n_box3.at[k - 1], p.peer("z", k))
            for k in range(1, NZ)
        ]

    def step(self, stage):
        p, r = self.p, self.link.r
        self.wait(stage)
        if stage == 0:
            r.n_sum[...] = r.g_norm[...] + r.n_box0[...]
        elif stage == 1:
            r.n_all[...] = r.n_sum[...] + r.n_box1[...]
        else:
            r.n_half[...] = r.n_all[:, p.b] + r.n_box2[...]
        self.start(stage + 1)

    def total(self):
        r = self.link.r
        return r.n_half[self.p.a] + ((r.n_box3[0] + r.n_box3[1]) + r.n_box3[2])


class ScatterEncoder(Stages):
    def __init__(self, link, place, share):
        super().__init__(link, (NY, 1))
        self.p, self.share = place, share
        self.boxes = (link.r.d_third, link.r.second_low)

    def rows(self, y, c):
        at = pl.multiple_of((y * NC + c) * self.share, self.share)
        return self.link.r.big1.at[:, pl.ds(at, self.share), :]

    def copies(self, stage):
        p, r, send, keys = self.p, self.link.r, self.link.send, self.keys[stage]
        if stage == 0:
            return [
                send(keys[y], self.rows(y, 1 - p.c), self.boxes[y], p.peer("core"))
                for y in range(NY)
            ]
        return [send(keys[0], self.rows(1 - p.y, p.c), r.e_box1, p.peer("y"))]

    def step(self):
        self.wait(0)
        for y in range(NY):
            ref = self.rows(y, self.p.c)
            for m in range(ref.shape[0]):
                ref[m] = ref[m] + self.boxes[y][m]
        self.start(1)

    def finish(self):
        self.wait(1)
        ref = self.rows(self.p.y, self.p.c)
        for m in range(ref.shape[0]):
            ref[m] = ref[m] + self.link.r.e_box1[m]
        return ref


class ShareFfn(Stages):
    def __init__(self, link, place, box):
        super().__init__(link, (3,))
        self.p, self.box = place, box

    def copies(self, stage):
        p, send, keys = self.p, self.link.send, self.keys[0]
        ref = self.box.at[p.t]
        axes = ("core", "y", "both")
        return [send(keys[i], ref, ref, p.peer(axes[i])) for i in range(3)]


def each(count, body, ticks=None):
    def step(i, carry):
        for k, tick in (ticks or {}).items():
            pl.when(i == k)(tick)
        body(i)
        return carry

    lax.fori_loop(0, count, step, 0)


SEMS = 115


def layer_kernel(names, groups, scale, *refs):
    r = Refs()
    for name, ref in zip(names, refs):
        setattr(r, name, ref)
    micro, r.share = r.stream.shape[0], r.stream.shape[1]
    r.slots = r.share // SLOT
    r.quads = r.stream.shape[2] // QUAD
    r.enc_len = r.encoder.shape[1]
    r.frame = frame_rows(r.share)
    p = Place(groups)
    link = Link(r)

    mine = pl.ds(pl.multiple_of(p.t * r.share, r.share), r.share)
    half = pl.ds(pl.multiple_of(p.t * (r.share // 2), r.share // 2), r.share // 2)
    pairs = [
        (r.self_query, r.w.at[SELF, p.y, p.c, p.a, p.b]),
        (r.self_key_value, r.w.at[pl.ds(SELF + 1, 2), p.y, p.c, p.a, p.b]),
        (r.cross_query, r.w.at[CROSS, p.y, p.c, p.a, p.b]),
        (r.cross_key_value, r.w.at[pl.ds(CROSS + 1, 2), p.y, p.c, p.a, p.b]),
    ]
    for k in range(4):
        up = pl.ds(pl.multiple_of(p.t * 512 + k * 128, 128), 128)
        pairs.append((r.ffn_in.at[:, up], r.w.at[UP + k, p.y, p.c, p.a, p.b]))
        down = pl.ds(pl.multiple_of(p.t * 128, 128), 128)
        pairs.append(
            (r.ffn_out.at[pl.ds(k * 64, 64), down], r.w.at[DOWN + k, p.y, p.c, p.a, p.b])
        )
    weights = len(pairs)
    pairs += [
        (r.stream_hbm.at[:, mine, :], r.stream),
        (r.context_hbm.at[:, mine, :], r.context),
        (r.masks_hbm.at[:, half, :], r.masks),
        (r.encoder, r.big1),
        (r.out_grad, r.cotangent),
    ]
    copies = [
        pltpu.make_async_copy(source, target, r.sems.at[i])
        for i, (source, target) in enumerate(pairs)
    ]
    for copy in copies:
        copy.start()
    partners = [p.peer("z", k) for k in range(1, NZ)]
    partners += [p.peer(axis) for axis in ("x", "y", "core", "both")]
    barrier = pltpu.get_barrier_semaphore()
    for device in partners:
        pl.semaphore_signal(barrier, inc=1, device_id=device, device_id_type=MESH)
    r.w[SELF + 3, p.y, p.c, p.a, p.b] = r.self_output[...].astype(F32).T.astype(BF16)
    r.w[CROSS + 3, p.y, p.c, p.a, p.b] = r.cross_output[...].astype(F32).T.astype(BF16)
    r.pack[p.a, p.b, 0:3, :64] = r.norm_gain[...].astype(F32)
    r.pack[p.a, p.b, 3:6, :64] = r.norm_bias[...].astype(F32)
    for copy in copies[:weights]:
        copy.wait()
    pl.semaphore_wait(barrier, len(partners))

    first = [Gather(link, p, SELF + k, 1, "xy" if k % 2 == 0 else "yx") for k in range(4)]
    rest = [Gather(link, p, CROSS + 2 * k, 2, "xy" if k % 2 == 0 else "yx") for k in range(6)]
    cross, up, down = rest[:2], rest[2:4], rest[4:]
    norms = GatherNorms(link, p)

    def start(items, stage):
        for item in items:
            item.start(stage)

    def move(items, stage):
        for item in items:
            item.wait(stage)
            item.start(stage + 1)

    def wait(items, stage):
        for item in items:
            item.wait(stage)

    start(first, 0)
    norms.start(0)
    move(first, 0)
    start(cross, 0)
    r.sums[...] = jnp.zeros(r.sums.shape, F32)
    move(first, 1)
    norms.wait(0)
    norms.start(1)
    move(first, 2)
    for copy in copies[weights:]:
        copy.wait()
    norms.wait(1)
    r.norms[...] = jnp.concatenate(
        [r.pack[d // NX, d % NX, :, :64] for d in range(NZ * NX)], axis=1
    )
    wait(first, 3)

    def self_tick0():
        move(cross, 0)
        start(up, 0)

    def self_tick1():
        move(cross, 1)
        move(up, 0)
        start(down, 0)

    def self_tick2():
        move(cross, 2)
        move(up, 1)
        move(down, 0)

    def self_tick3():
        move(up, 2)
        move(down, 1)

    each(
        micro,
        functools.partial(forward_self, r),
        {0: self_tick0, 1: self_tick1, 2: self_tick2, 3: self_tick3},
    )
    wait(cross, 3)
    each(micro, functools.partial(forward_cross, r), {1: lambda: move(down, 2)})
    wait(up, 3)
    wait(down, 3)
    for item in link.all:
        item.drain()
    link.all = []
    each(micro, functools.partial(feed_forward, r))
    out = [pltpu.make_async_copy(r.d_first, r.block_out, r.sems.at[0])]
    out[0].start()
    each(4, functools.partial(ffn_grads, r))

    sums = {}
    for name, (kind, count, order) in SCATTERS.items():
        boxes = [getattr(r, "box_" + name + str(i)) for i in range(4)]
        sums[name] = Scatter(link, p, kind, count, order, boxes)
    norm_sums = ScatterNorms(link, p)
    rows = ScatterEncoder(link, p, r.share)
    share_up, share_down = ShareFfn(link, p, r.all_up), ShareFfn(link, p, r.all_down)

    sums["up"].start(0)
    sums["down"].start(0)
    clear_pads(r)
    out[0].wait()

    def cross_tick1():
        sums["up"].step(0)
        sums["down"].step(0)

    each(
        micro,
        functools.partial(backward_cross, r),
        {1: cross_tick1, 3: lambda: sums["up"].step(1)},
    )
    rows.start(0)
    for d in range(NZ * NX):
        r.g_norm[d // NX, d % NX] = jnp.zeros(r.g_norm.shape[2:], F32)
        r.g_norm[d // NX, d % NX, :, :64] = r.sums[:, d * 64 : (d + 1) * 64]
    norm_sums.start(0)
    cross_grads(r)
    sums["cross"].start(0)
    output_grads(r)
    sums["mix"].start(0)
    rows.step()
    sums["down"].step(1)

    def share_sum(name, box, item):
        item_sum = sums[name]
        item_sum.wait(3)
        for k in range(4):
            box[p.t, k] = item_sum.total(k).astype(BF16)
        item.start(0)

    def back_tick0():
        sums["up"].step(2)
        sums["cross"].step(0)
        sums["mix"].step(0)

    def back_tick1():
        sums["down"].step(2)
        norm_sums.step(0)

    def back_tick2():
        share_sum("up", r.all_up, share_up)
        sums["mix"].step(1)
        norm_sums.step(1)

    def back_tick3():
        share_sum("down", r.all_down, share_down)
        sums["cross"].step(1)
        norm_sums.step(2)

    each(
        micro,
        functools.partial(backward_self, r),
        {0: back_tick0, 1: back_tick1, 2: back_tick2, 3: back_tick3},
    )
    out = [
        pltpu.make_async_copy(r.cotangent, r.stream_grad, r.sems.at[0]),
        pltpu.make_async_copy(r.second_low, r.context_grad, r.sems.at[1]),
    ]
    for copy in out:
        copy.start()
    self_grads(r)
    sums["query"].start(0)
    sums["pair"].start(0)
    ready = rows.finish()
    out.append(pltpu.make_async_copy(ready, r.encoder_grad, r.sems.at[2]))
    out[2].start()
    sums["cross"].step(2)
    sums["mix"].step(2)
    sums["query"].step(0)
    sums["pair"].step(0)
    sums["query"].step(1)
    sums["pair"].step(1)
    sums["query"].step(2)
    sums["pair"].step(2)
    share_up.wait(0)
    for t in range(NY * NC):
        for k in range(4):
            at = t * 512 + k * 128
            r.grad_ffn_in[:, at : at + 128] = r.all_up[t, k].astype(F32) * scale
    share_down.wait(0)
    for t in range(NY * NC):
        for n in range(2):
            block = jnp.concatenate([r.all_down[t, n], r.all_down[t, 2 + n]], axis=0)
            r.grad_ffn_out[n * 128 : (n + 1) * 128, t * 128 : (t + 1) * 128] = (
                block.astype(F32) * scale
            ).T
    norm_sums.wait(3)
    total = norm_sums.total() * scale
    r.grad_norm_gain[...] = total[0:3, :64]
    r.grad_norm_bias[...] = total[3:6, :64]
    sums["cross"].wait(3)
    r.grad_cross_query[...] = sums["cross"].total(0) * scale
    r.grad_cross_key_value[0] = sums["cross"].total(1) * scale
    r.grad_cross_key_value[1] = sums["cross"].total(2) * scale
    r.grad_cross_output[...] = (sums["cross"].total(3) * scale).T
    sums["mix"].wait(3)
    r.grad_self_output[...] = (sums["mix"].total(0) * scale).T
    sums["query"].wait(3)
    r.grad_self_query[...] = sums["query"].total(0) * scale
    sums["pair"].wait(3)
    r.grad_self_key_value[0] = sums["pair"].total(0) * scale
    r.grad_self_key_value[1] = sums["pair"].total(1) * scale
    for item in link.all:
        item.drain()
    for copy in out:
        copy.wait()


def vmem():
    return pl.BlockSpec(memory_space=pltpu.VMEM)


def hbm():
    return pl.BlockSpec(memory_space=pl.ANY)


WEIGHTS = (
    "self_query", "self_key_value", "self_output",
    "cross_query", "cross_key_value", "cross_output",
    "ffn_in", "ffn_out", "norm_gain", "norm_bias",
)


def layer(groups, scale, stream, context, encoder, masks, table, out_grad, weights):
    micro, row, width = stream.shape
    share = out_grad.shape[1]
    enc_len = encoder.shape[1]
    frame, wide = frame_rows(share), window_rows()
    slots, quads = share // SLOT, width // QUAD
    small = ("self_output", "cross_output", "norm_gain", "norm_bias")
    ins = [
        ("stream_hbm", stream, hbm()),
        ("context_hbm", context, hbm()),
        ("encoder", encoder, hbm()),
        ("masks_hbm", masks, hbm()),
        ("table", table, pl.BlockSpec(memory_space=pltpu.SMEM)),
        ("out_grad", out_grad, hbm()),
    ]
    for name, value in zip(WEIGHTS, weights):
        ins.append((name, value, vmem() if name in small else hbm()))
    part = jax.ShapeDtypeStruct((micro, share, width), BF16)
    outs = [
        ("block_out", part, hbm()),
        ("stream_grad", part, hbm()),
        ("context_grad", part, hbm()),
        ("encoder_grad", part, hbm()),
    ]
    for name, value in zip(WEIGHTS, weights):
        outs.append(("grad_" + name, jax.ShapeDtypeStruct(value.shape, F32), vmem()))
    low = pltpu.VMEM((micro, share, width), BF16)
    high = pltpu.VMEM((micro, share, width), F32)
    window = pltpu.VMEM((micro, frame, width), BF16)
    big = pltpu.VMEM((micro, enc_len, width), BF16)
    norm = pltpu.VMEM((NZ, NX, 8, 128), F32)
    scratch = [
        ("w", pltpu.VMEM((16, NY, NC, NZ, NX, 64, 128), BF16)),
        ("g_ffn", pltpu.VMEM((8, NY, NC, NZ, NX, 64, 128), BF16)),
        ("stream", low),
        ("context", low),
        ("cotangent", low),
        ("masks", pltpu.VMEM((micro, share // 2, 128), jnp.int32)),
        ("q_self", low),
        ("k_self", low),
        ("v_self", low),
        ("mixed_self", low),
        ("first_low", low),
        ("q_cross", low),
        ("k_cross", window),
        ("v_cross", window),
        ("source", window),
        ("mixed_cross", low),
        ("second_low", low),
        ("d_third", low),
        ("d_second", low),
        ("d_first", low),
        ("p_self", pltpu.VMEM((micro, slots, quads, SLOT, QUAD), BF16)),
        ("p_cross", pltpu.VMEM((micro, slots, quads, wide, QUAD), BF16)),
        ("residual", high),
        ("normed1", low),
        ("normed2", low),
        ("factor", pltpu.VMEM((micro, share, 2), F32)),
        ("big1", big),
        ("big2", big),
        ("shifted", pltpu.VMEM((2 * enc_len - frame, width), BF16)),
        ("norms", pltpu.VMEM((8, width), F32)),
        ("sums", pltpu.VMEM((8, width), F32)),
        ("pack", norm),
        ("g_norm", norm),
        ("n_sum", norm),
        ("n_all", norm),
        ("n_half", pltpu.VMEM((NZ, 8, 128), F32)),
        ("n_box0", norm),
        ("n_box1", norm),
        ("n_box2", pltpu.VMEM((NZ, 8, 128), F32)),
        ("n_box3", pltpu.VMEM((NZ - 1, 8, 128), F32)),
        ("e_box1", low),
        ("all_up", pltpu.VMEM((NY * NC, 4, 64, 128), BF16)),
        ("all_down", pltpu.VMEM((NY * NC, 4, 64, 128), BF16)),
        ("sems", pltpu.SemaphoreType.DMA((17,))),
        ("send_sems", pltpu.SemaphoreType.DMA((SEMS,))),
        ("recv_sems", pltpu.SemaphoreType.DMA((SEMS,))),
    ]
    for name, (_, count, order) in SCATTERS.items():
        scratch += scatter_boxes("box_" + name, count, order)
    names = [item[0] for item in ins + outs + scratch]
    return pl.pallas_call(
        functools.partial(layer_kernel, names, groups, scale),
        out_shape=[item[1] for item in outs],
        in_specs=[item[2] for item in ins],
        out_specs=[item[2] for item in outs],
        scratch_shapes=[item[1] for item in scratch],
        compiler_params=pltpu.CompilerParams(
            vmem_limit_bytes=VMEM_LIMIT, collective_id=0, has_side_effects=True
        ),
        cost_estimate=pl.CostEstimate(
            flops=30_000_000_000, bytes_accessed=30_000_000, transcendentals=4_000_000
        ),
    )(*[item[1] for item in ins])


GATHER_DIM = (0, 1, 1, 0, 1, 1, 0, 0, 1, 1)


def per_device(
    query_stream,
    context_stream,
    encoder_out,
    query_masks,
    source_segments,
    out_grad,
    *weights,
):
    micro, row, width = query_stream.shape
    share = out_grad.shape[1]
    slots = share // SLOT
    t = lax.axis_index("tensor")
    replicas = lax.axis_size("dp")
    scale = float(micro * row * replicas) ** (-0.5)
    groups = replicas // (NZ * NX)
    near = [[i * groups + j for j in range(groups)] for i in range(NZ * NX)]
    if groups > 1:
        weights = [
            lax.all_gather(item, "dp", axis=dim, tiled=True, axis_index_groups=near)
            for item, dim in zip(weights, GATHER_DIM)
        ]
    bounds = t * slots + jnp.arange(slots + 1, dtype=jnp.int32)
    starts = jnp.sum(
        (source_segments < bounds[None, :, None]).astype(jnp.int32), axis=-1
    )
    table = window_table(starts, share, encoder_out.shape[1])
    results = layer(
        groups, scale, query_stream, context_stream, encoder_out, query_masks, table,
        out_grad, weights,
    )
    grads = results[4:]
    if groups > 1:
        grads = [
            lax.psum_scatter(
                item, "dp", scatter_dimension=dim, tiled=True, axis_index_groups=near
            )
            for item, dim in zip(grads, GATHER_DIM)
        ]
    return (*results[:4], *grads)


def solution(mesh):
    in_specs = (
        P(None, "dp", None),
        P(None, "dp", None),
        P(None, "dp", None),
        P(None, "dp", None),
        P(None, "dp", None),
        P(None, ("dp", "tensor"), None),
        P("dp", "tensor"),
        P(None, "dp", "tensor"),
        P("tensor", "dp"),
        P("dp", "tensor"),
        P(None, "dp", "tensor"),
        P("tensor", "dp"),
        P("dp", None),
        P("dp", None),
        P(None, "dp"),
        P(None, "dp"),
    )
    out_specs = (
        P(None, ("dp", "tensor"), None),
        P(None, ("dp", "tensor"), None),
        P(None, ("dp", "tensor"), None),
        P(None, ("dp", "tensor"), None),
        P("dp", "tensor"),
        P(None, "dp", "tensor"),
        P("tensor", "dp"),
        P("dp", "tensor"),
        P(None, "dp", "tensor"),
        P("tensor", "dp"),
        P("dp", None),
        P("dp", None),
        P(None, "dp"),
        P(None, "dp"),
    )
    return jax.shard_map(
        per_device, mesh=mesh, in_specs=in_specs, out_specs=out_specs, check_vma=False
    )
```

time: 1900 us -> 199 us (0.10)
  waiting for transfers between devices: 1110 us -> 0 us
  matrix products: 232 us -> 0 us
  blocking collectives: 228 us -> 0 us
  Pallas kernels: 0 us -> 177 us
  local copies, waits for them, and re-layouts: 165 us -> 19.6 us
  other arithmetic: 118 us -> 0.56 us
  between operations: 21.2 us -> 0.73 us
    reduce_scatter x28 -> x0, waiting for transfers between devices: 732 us -> none  [the longest x4 106 us: back_self(): lax.psum_scatter(terms[1].astype(jnp.bfloat16), 'tensor', scatter_dimensi...]
    unnamed x53 -> x0, waiting for transfers between devices: 264 us -> none
    dot_general x192 -> x0, matrix products: 232 us -> none  [the longest x40 62.4 us: back_project(): jnp.einsum('te,de->td', gradient, weight, preferred_element_type=jnp.floa...]
    all_gather x8 -> x0, blocking collectives: 223 us -> none  [the longest x1 32.7 us: gather_shards(): lax.all_gather(shards[1], 'dp', axis=1, tiled=True)]
    pallas_call x0 -> x1, Pallas kernels: none -> 177 us  [layer(): pl.pallas_call(functools.partial(layer_kernel, names, groups, scale), out...]
    all_gather x14 -> x0, waiting for transfers between devices: 82.2 us -> none  [the longest x1 46.5 us: gather_shards(): lax.all_gather(shards[7], 'dp', axis=0, tiled=True)]
    scatter-add x8 -> x0, other arithmetic: 35.6 us -> none  [fold_window(): summed = jax.ops.segment_sum(pieces, targets, num_segments=block_total)]
    psum x1 -> x0, waiting for transfers between devices: 34 us -> none  [per_device(): lax.psum(summed[6].astype(jnp.bfloat16), 'tensor').astype(jnp.float32)]
  transfers between devices with their start and end apart: 48 -> 0, of which waited for: 34 -> 0; matrix products, arithmetic and copies ran while one was open for 23% -> 0% of each run, Pallas kernels for 0% -> 0%
where the time goes in v1:
time: 199 us; the launch traced here: 198 us
  Pallas kernels  177 us (89%)
  local copies, waits for them, and re-layouts  19.6 us (10%)
    pallas_call x1, Pallas kernels, layer(): pl.pallas_call(functools.partial(layer_kernel, names, groups, scale), out...  177 us
    unnamed x38, local copies, waits for them, and re-layouts  15.7 us

profile of v1, /device:TPU:0, one launch (start us, length us, event | category | flops | bytes accessed | tf_op | source)
XLA Modules:
  0.0 198.2 jit_solution(16101572399766398041)
XLA Ops:
  0.7 0.7 copy.50
  1.4 0.3 convert_reduce_fusion
  1.7 0.1 copy.48
  1.8 0.1 copy.46
  1.8 0.1 fusion.17
  2.0 0.1 copy.47
  2.1 0.1 add_select_fusion
  2.2 0.1 add_subtract_fusion
  2.2 0.7 concatenate.3.refs_4_
  2.9 1.4 copy.41.refs_8_
  4.3 1.4 copy.42.refs_11_
  5.8 177.3 %shard_map.263 = (bf16[4,256,512]{2,1,0:T(8,128)(2,1)}, bf16[4,256,512]{2,1,0:T(8,128)(2,1)}, bf16[4,256,512]{2,1,0:T(8,128)(2,1)}, bf16[4,256,512]{2,1,0:T(8,12...) custom-call(bf16[4,1024,512]{2,1,0:T(8,128)(2,1)} %refs_0_.1, ...), custom_call_target="tpu_custom_call" | custom-call | flops 30000001024 | bytes 30000000 | tf_op jit(solution)/shard_map/pallas_call | solution.py:1018
  183.1 0.0 copy-start.1
  183.1 0.0 copy-start
  183.1 1.7 copy.43
  184.8 1.5 copy.44
  186.3 0.0 copy-start.7
  186.3 0.0 copy-start.5
  186.3 0.0 copy-start.6
  186.3 0.0 copy-start.4
  186.3 0.0 copy-start.3
  186.3 2.3 %copy.63 = bf16[4,256,512]{2,1,0:T(8,128)(2,1)} copy(bf16[4,256,512]{2,1,0:T(8,128)(2,1)} %get-tuple-element.81) | data formatting | bytes 2097152
  188.7 0.0 copy-start.2
  188.7 0.0 copy-start.9
  188.7 0.0 copy-start.8
  188.7 2.3 %copy.64 = bf16[4,256,512]{2,1,0:T(8,128)(2,1)} copy(bf16[4,256,512]{2,1,0:T(8,128)(2,1)} %get-tuple-element.82) | data formatting | bytes 2097152
  191.0 0.0 copy-done.1
  191.0 1.0 copy.65
  192.0 0.0 copy-done
  192.0 1.0 copy.66
  192.9 0.0 copy-done.7
  192.9 0.6 copy.67
  193.5 0.0 copy-done.5
  193.6 0.6 copy.68
  194.2 0.0 copy-done.6
  194.2 0.6 copy.69
  194.8 0.0 copy-done.4
  194.8 0.6 copy.70
  195.4 0.0 copy-done.3
  195.4 0.8 copy.71
  196.2 0.0 copy-done.2
  196.2 0.8 copy.72
  197.0 0.0 copy-done.9
  197.0 0.6 copy.73
  197.6 0.0 copy-done.8
  197.6 0.6 copy.74
  (4 shorter events, 0.0 us)
Async XLA Ops:
  183.1 7.9 %copy-start.1 = (bf16[4,256,512]{2,1,0:T(8,128)(2,1)S(1)}, bf16[4,256,512]{2,1,0:T(8,128)(2,1)}, u32[]{:S(2)}) copy-start(bf16[4,256,512]{2,1,0:T(8,128)(2,1)} %get-tuple-element.83) | copy-start | bytes 3145732
  183.1 8.9 %copy-start = (bf16[4,256,512]{2,1,0:T(8,128)(2,1)S(1)}, bf16[4,256,512]{2,1,0:T(8,128)(2,1)}, u32[]{:S(2)}) copy-start(bf16[4,256,512]{2,1,0:T(8,128)(2,1)} %get-tuple-element.84) | copy-start | bytes 3145732
  186.3 6.6 %copy-start.7 = (f32[64,128]{1,0:T(8,128)S(1)}, f32[64,128]{1,0:T(8,128)}, u32[]{:S(2)}) copy-start(f32[64,128]{1,0:T(8,128)} %get-tuple-element.85) | copy-start | bytes 98308
  186.3 7.2 %copy-start.5 = (f32[2,64,128]{2,1,0:T(8,128)S(1)}, f32[2,64,128]{2,1,0:T(8,128)}, u32[]{:S(2)}) copy-start(f32[2,64,128]{2,1,0:T(8,128)} %get-tuple-element.86) | copy-start | bytes 196612
  186.3 7.9 %copy-start.6 = (f32[64,128]{1,0:T(8,128)S(1)}, f32[64,128]{1,0:T(8,128)}, u32[]{:S(2)}) copy-start(f32[64,128]{1,0:T(8,128)} %get-tuple-element.88) | copy-start | bytes 98308
  186.3 8.5 %copy-start.4 = (f32[2,64,128]{2,1,0:T(8,128)S(1)}, f32[2,64,128]{2,1,0:T(8,128)}, u32[]{:S(2)}) copy-start(f32[2,64,128]{2,1,0:T(8,128)} %get-tuple-element.89) | copy-start | bytes 196612
  186.3 9.1 %copy-start.3 = (f32[64,2048]{1,0:T(8,128)S(1)}, f32[64,2048]{1,0:T(8,128)}, u32[]{:S(2)}) copy-start(f32[64,2048]{1,0:T(8,128)} %get-tuple-element.91) | copy-start | bytes 1572868
  188.7 7.6 %copy-start.2 = (f32[256,512]{1,0:T(8,128)S(1)}, f32[256,512]{1,0:T(8,128)}, u32[]{:S(2)}) copy-start(f32[256,512]{1,0:T(8,128)} %get-tuple-element.92) | copy-start | bytes 1572868
  188.7 8.4 %copy-start.9 = (f32[3,64]{1,0:T(4,128)S(1)}, f32[3,64]{1,0:T(4,128)}, u32[]{:S(2)}) copy-start(f32[3,64]{1,0:T(4,128)} %get-tuple-element.93) | copy-start | bytes 2308
  188.7 8.9 %copy-start.8 = (f32[3,64]{1,0:T(4,128)S(1)}, f32[3,64]{1,0:T(4,128)}, u32[]{:S(2)}) copy-start(f32[3,64]{1,0:T(4,128)} %get-tuple-element.94) | copy-start | bytes 2308

commit v2 on v1

v2 whole, which is shorter than its diff:
```python
import functools

import jax
import jax.numpy as jnp
from jax import lax
from jax.experimental import pallas as pl
from jax.experimental.pallas import tpu as pltpu
from jax.sharding import PartitionSpec as P

HEAD_DIM = 64
SLOT = 64
SEG_MOST = 128
QUAD = 4 * HEAD_DIM
PAIR = 2 * HEAD_DIM
NZ, NX, NY, NC = 4, 2, 2, 2
PIECE = 2
SELF, CROSS, FEED, KINDS = 0, 4, 8, 16
BF16 = jnp.bfloat16
F32 = jnp.float32
MESH = pl.DeviceIdType.MESH
DP, TENSOR = "dp", "tensor"

epsilon = 1e-05
neg_fill = -1e30
gelu_coef = 0.7978845608028654
gelu_cube = 0.044715
VMEM_LIMIT = 65400 * 1024


def mm(left, right):
    return jnp.dot(left, right, preferred_element_type=F32)


def mm_nt(left, right):
    return lax.dot_general(left, right, (((1,), (1,)), ((), ())), preferred_element_type=F32)


def mm_tn(left, right):
    return lax.dot_general(left, right, (((0,), (0,)), ((), ())), preferred_element_type=F32)


def norm_forward(value, gain, bias):
    center = jnp.mean(value, axis=-1, keepdims=True)
    shifted = value - center
    factor = lax.rsqrt(jnp.mean(shifted * shifted, axis=-1, keepdims=True) + epsilon)
    normed = shifted * factor
    return normed * gain + bias, normed, factor


def norm_backward(incoming, normed, factor, gain):
    scaled = incoming * gain
    inside = (
        scaled
        - jnp.mean(scaled, axis=-1, keepdims=True)
        - normed * jnp.mean(scaled * normed, axis=-1, keepdims=True)
    )
    return (
        factor * inside,
        jnp.sum(incoming * normed, axis=0, keepdims=True),
        jnp.sum(incoming, axis=0, keepdims=True),
    )


def columns(r, kind):
    parts = [r.w[kind, t // NC, t % NC].reshape(-1, 128) for t in range(NY * NC)]
    return jnp.concatenate(parts, axis=1)


def grad_place(r, kind):
    if kind >= FEED:
        return r.g_ffn, kind - FEED
    return r.w, kind + FEED


def store_columns(ref, at, value):
    for t in range(NY * NC):
        ref[at, t // NC, t % NC] = value[:, t * 128 : (t + 1) * 128].reshape(NZ, NX, -1, 128)


def head_marks():
    lane = lax.broadcasted_iota(jnp.int32, (1, QUAD), 1) // HEAD_DIM
    return [jnp.where(lane == h, 1.0, 0.0).astype(BF16) for h in range(4)]


def spread_heads(rows, marks):
    return jnp.concatenate([rows * mark for mark in marks], axis=0)


def fold_pairs(weights, rows):
    first = lax.broadcasted_iota(jnp.int32, (SLOT, PAIR), 1) < HEAD_DIM
    parts = []
    for p in range(2):
        cut = slice(p * PAIR, (p + 1) * PAIR)
        full = mm_tn(weights[:, cut], rows[:, cut])
        parts.append(jnp.where(first, full[:SLOT], full[SLOT:]))
    return jnp.concatenate(parts, axis=1)


def soft_keys(scores, allowed):
    scores = jnp.where(allowed, scores, neg_fill)
    top = jnp.max(scores, axis=0, keepdims=True)
    raised = jnp.exp(scores - top)
    return (raised * (1.0 / jnp.sum(raised, axis=0, keepdims=True))).astype(BF16)


def attend_back(items, marks):
    d_spread = [spread_heads(item[4], marks) for item in items]
    d_probs = [mm_nt(item[2], spread) for item, spread in zip(items, d_spread)]
    d_values = [mm(item[0], spread).astype(BF16) for item, spread in zip(items, d_spread)]
    d_scores = []
    for item, d_prob in zip(items, d_probs):
        wide = item[0].astype(F32)
        inner = jnp.sum(wide * d_prob, axis=0, keepdims=True)
        d_scores.append((wide * (d_prob - inner)).astype(BF16))
    d_keys = [
        mm(d_score, spread_heads(item[3], marks)).astype(BF16)
        for item, d_score in zip(items, d_scores)
    ]
    d_queries = [
        (fold_pairs(d_score, item[1]) * HEAD_DIM ** (-0.5)).astype(BF16)
        for item, d_score in zip(items, d_scores)
    ]
    return d_queries, d_keys, d_values


def cut(value, s, g):
    return value[s * SLOT : (s + 1) * SLOT, g * QUAD : (g + 1) * QUAD]


class Refs:
    pass


def frame_rows(share):
    return (share // SLOT) * SEG_MOST + 16


def window_rows():
    return SEG_MOST + 16


def window_table(starts, share, enc_len):
    frame, wide = frame_rows(share), window_rows()
    base = jnp.minimum(starts[:, :1] // 16 * 16, enc_len - frame)
    begin = starts[:, :-1] - base
    at = jnp.minimum(begin // 16 * 16, frame - wide)
    low = begin - at
    high = low + starts[:, 1:] - starts[:, :-1]
    return jnp.concatenate(
        [base // 16, (enc_len - frame - base) // 16, at // 16, low, high, (frame - wide - at) // 16],
        axis=1,
    )


def frame_start(r, m):
    return r.table[m, 0] * 16


def slot_window(r, m, s):
    at = r.table[m, 2 + s] * 16
    return at, r.table[m, 2 + r.slots + s], r.table[m, 2 + 2 * r.slots + s]


def slot_shift(r, m, s):
    return r.table[m, 2 + 3 * r.slots + s] * 16


def forward_self(r, m):
    marks = head_marks()
    stream, context = r.stream[m], r.context[m]
    queries = (mm(stream, columns(r, SELF + 0)) * HEAD_DIM ** (-0.5)).astype(BF16)
    keys = mm(context, columns(r, SELF + 1)).astype(BF16)
    values = mm(context, columns(r, SELF + 2)).astype(BF16)
    r.q_self[m], r.k_self[m], r.v_self[m] = queries, keys, values
    row = lax.broadcasted_iota(jnp.int32, (SLOT, QUAD), 0)
    lane = lax.broadcasted_iota(jnp.int32, (SLOT, QUAD), 1) % SLOT
    place = jnp.where(lane == 2 * (row % 32) + row // 32, 1.0, 0.0).astype(BF16)
    units = [(s, g) for s in range(r.slots) for g in range(r.quads)]
    allowed = []
    for s in range(r.slots):
        bits = r.masks[m, s * 32 : (s + 1) * 32].astype(F32)
        bits = jnp.concatenate([bits[:, :SLOT], bits[:, SLOT:]], axis=0).astype(BF16)
        allowed.append(mm_tn(bits, place) > 0.5)
    scores = [mm_nt(cut(keys, s, g), spread_heads(cut(queries, s, g), marks)) for s, g in units]
    probs = [soft_keys(score, allowed[s]) for score, (s, g) in zip(scores, units)]
    mixed = [fold_pairs(prob, cut(values, s, g)).astype(BF16) for prob, (s, g) in zip(probs, units)]
    for prob, one, (s, g) in zip(probs, mixed, units):
        r.p_self[m, s, g] = prob
        r.mixed_self[m, s * SLOT : (s + 1) * SLOT, g * QUAD : (g + 1) * QUAD] = one


def first_norm(r, m):
    attn = mm_nt(r.mixed_self[m], columns(r, SELF + 3))
    first, normed, factor = norm_forward(
        r.stream[m].astype(F32) + attn, r.norms[0:1, :], r.norms[3:4, :]
    )
    r.residual[m], r.factor[m, :, 0:1] = first, factor
    r.normed1[m] = normed.astype(BF16)
    r.first_low[m] = first.astype(BF16)


def forward_cross(r, m):
    marks = head_marks()
    base = frame_start(r, m)
    source = r.big1[m, pl.ds(base, r.frame), :]
    r.source[m] = source
    r.k_cross[m] = mm(source, columns(r, CROSS + 1)).astype(BF16)
    r.v_cross[m] = mm(source, columns(r, CROSS + 2)).astype(BF16)
    queries = (mm(r.first_low[m], columns(r, CROSS + 0)) * HEAD_DIM ** (-0.5)).astype(BF16)
    r.q_cross[m] = queries
    wide = window_rows()
    row = lax.broadcasted_iota(jnp.int32, (wide, QUAD), 0)
    units = [(s, g) for s in range(r.slots) for g in range(r.quads)]
    windows = [slot_window(r, m, s) for s in range(r.slots)]
    allowed = [(row >= low) & (row < high) for _, low, high in windows]

    def view(ref, s, g):
        return ref[m, pl.ds(windows[s][0], wide), g * QUAD : (g + 1) * QUAD]

    scores = [
        mm_nt(view(r.k_cross, s, g), spread_heads(cut(queries, s, g), marks)) for s, g in units
    ]
    probs = [soft_keys(score, allowed[s]) for score, (s, g) in zip(scores, units)]
    mixed = [
        fold_pairs(prob, view(r.v_cross, s, g)).astype(BF16) for prob, (s, g) in zip(probs, units)
    ]
    for prob, (s, g) in zip(probs, units):
        r.p_cross[m, s, g] = prob
    mixed = jnp.concatenate(
        [
            jnp.concatenate(mixed[s * r.quads : (s + 1) * r.quads], axis=1)
            for s in range(r.slots)
        ],
        axis=0,
    )
    r.mixed_cross[m] = mixed
    attn = mm_nt(mixed, columns(r, CROSS + 3))
    second, normed, factor = norm_forward(
        r.residual[m] + attn, r.norms[1:2, :], r.norms[4:5, :]
    )
    r.residual[m], r.factor[m, :, 1:2] = second, factor
    r.normed2[m] = normed.astype(BF16)
    r.second_low[m] = second.astype(BF16)


def tokens(ref):
    value = ref[...]
    return value.reshape(-1, value.shape[-1])


def pieces(r, i):
    return pl.ds(i * PIECE, PIECE), pl.ds(pl.multiple_of(i * PIECE * r.share, 512), PIECE * r.share)


def feed(r, i):
    j = lax.div(i, r.halves)
    some, rows = pieces(r, lax.rem(i, r.halves))
    low = tokens(r.second_low.at[some])
    up, down = columns(r, FEED + 2 * j), columns(r, FEED + 2 * j + 1)
    for at in range(0, 512, 256):
        inner = mm(low, up[:, at : at + 256])
        square = inner * inner
        bent = jnp.tanh(gelu_coef * inner * (1.0 + gelu_cube * square))
        half = 0.5 * (1.0 + bent)
        r.big1[j, rows, at : at + 256] = (inner * half).astype(BF16)
        slope = half + 0.5 * inner * (1.0 - bent * bent) * gelu_coef * (
            1.0 + 3.0 * gelu_cube * square
        )
        r.big2[j, rows, at : at + 256] = slope.astype(BF16)
    r.residual[some] += mm(r.big1[j, rows, :], down).reshape(PIECE, r.share, -1)


def third_norm(r, m):
    result, normed, factor = norm_forward(r.residual[m], r.norms[2:3, :], r.norms[5:6, :])
    r.d_first[m] = result.astype(BF16)
    d_third, gain, bias = norm_backward(
        r.cotangent[m].astype(F32), normed, factor, r.norms[2:3, :]
    )
    r.sums[2:3, :] += gain
    r.sums[5:6, :] += bias
    r.d_third[m] = d_third.astype(BF16)
    r.residual[m] = d_third


def feed_back(r, j):
    up, down = columns(r, FEED + 2 * j), columns(r, FEED + 2 * j + 1)
    for i in range(r.halves):
        some, rows = pieces(r, i)
        slope = r.big2[j, rows, :].astype(F32)
        d_inner = (mm_nt(tokens(r.d_third.at[some]), down) * slope).astype(BF16)
        r.big2[j, rows, :] = d_inner
        r.residual[some] += mm_nt(d_inner, up).reshape(PIECE, r.share, -1)


def feed_grad(r, j):
    store_columns(r.g_ffn, 2 * j, mm_tn(tokens(r.second_low), r.big2[j]).astype(BF16))
    store_columns(r.g_ffn, 2 * j + 1, mm_tn(r.big1[j], tokens(r.d_third)).astype(BF16))


def second_back(r, m):
    d_cross, gain, bias = norm_backward(
        r.residual[m], r.normed2[m].astype(F32), r.factor[m, :, 1:2], r.norms[1:2, :]
    )
    r.sums[1:2, :] += gain
    r.sums[4:5, :] += bias
    r.residual[m] = d_cross
    r.d_second[m] = d_cross.astype(BF16)


def clear_pads(r):
    for s in range(r.slots):
        r.big2[s] = jnp.zeros(r.big2.shape[1:], BF16)


def backward_cross(r, m):
    marks = head_marks()
    wide = window_rows()
    reach = r.frame - wide
    d_mixed = mm(r.d_second[m], columns(r, CROSS + 3)).astype(BF16)
    queries = r.q_cross[m]
    windows = [slot_window(r, m, s) for s in range(r.slots)]

    def view(ref, s, g):
        return ref[m, pl.ds(windows[s][0], wide), g * QUAD : (g + 1) * QUAD]

    d_queries = []
    for g in range(r.quads):
        d_q, d_k, d_v = attend_back(
            [
                (
                    r.p_cross[m, s, g],
                    view(r.k_cross, s, g),
                    view(r.v_cross, s, g),
                    cut(queries, s, g),
                    cut(d_mixed, s, g),
                )
                for s in range(r.slots)
            ],
            marks,
        )
        for s in range(r.slots):
            r.big2[s, reach : reach + wide, :QUAD] = d_k[s]
            r.big2[s, reach : reach + wide, QUAD:] = d_v[s]
        total = None
        for s in range(r.slots):
            piece = r.big2[s, pl.ds(slot_shift(r, m, s), r.frame), :]
            total = piece if total is None else total + piece
        r.k_cross[m, :, g * QUAD : (g + 1) * QUAD] = total[:, :QUAD]
        r.v_cross[m, :, g * QUAD : (g + 1) * QUAD] = total[:, QUAD:]
        d_queries.append(jnp.concatenate(d_q, axis=0))
    d_queries = jnp.concatenate(d_queries, axis=1)
    r.q_cross[m] = d_queries
    d_first = r.residual[m] + mm_nt(d_queries, columns(r, CROSS + 0))
    d_attn, gain, bias = norm_backward(d_first, r.normed1[m].astype(F32), r.factor[m, :, 0:1], r.norms[0:1, :])
    r.sums[0:1, :] += gain
    r.sums[3:4, :] += bias
    r.residual[m] = d_attn
    r.d_first[m] = d_attn.astype(BF16)
    source_term = mm_nt(r.k_cross[m], columns(r, CROSS + 1)) + mm_nt(
        r.v_cross[m], columns(r, CROSS + 2)
    )
    low, edge, half = source_term.astype(BF16), r.enc_len - r.frame, r.enc_len // 2
    shift = r.table[m, 1] * 16
    r.big2[0, reach:edge, :] = jnp.zeros((edge - reach, low.shape[1]), BF16)
    r.big2[0, edge:, :] = low
    r.big2[1, : r.frame, :] = low
    r.big1[m, :half, :] = r.big2[0, pl.ds(shift, half), :]
    r.big1[m, half:, :] = r.big2[1, pl.ds(shift + (half - edge), half), :]
    r.big2[0, edge:, :] = jnp.zeros_like(low)
    r.big2[1, : r.frame, :] = jnp.zeros_like(low)


def backward_self(r, m):
    marks = head_marks()
    d_mixed = mm(r.d_first[m], columns(r, SELF + 3)).astype(BF16)
    queries, keys, values = r.q_self[m], r.k_self[m], r.v_self[m]
    units = [(s, g) for s in range(r.slots) for g in range(r.quads)]
    parts = attend_back(
        [
            (
                r.p_self[m, s, g],
                cut(keys, s, g),
                cut(values, s, g),
                cut(queries, s, g),
                cut(d_mixed, s, g),
            )
            for s, g in units
        ],
        marks,
    )
    d_q, d_k, d_v = [
        jnp.concatenate([jnp.concatenate(part[g :: r.quads], axis=0) for g in range(r.quads)], axis=1)
        for part in parts
    ]
    r.q_self[m], r.k_self[m], r.v_self[m] = d_q, d_k, d_v
    r.cotangent[m] = (r.residual[m] + mm_nt(d_q, columns(r, SELF + 0))).astype(BF16)
    r.second_low[m] = (
        mm_nt(d_k, columns(r, SELF + 1)) + mm_nt(d_v, columns(r, SELF + 2))
    ).astype(BF16)


def weight_grad(r, kind):
    left, right = {
        SELF: (r.stream, r.q_self),
        SELF + 1: (r.context, r.k_self),
        SELF + 2: (r.context, r.v_self),
        SELF + 3: (r.d_first, r.mixed_self),
        CROSS: (r.first_low, r.q_cross),
        CROSS + 1: (r.source, r.k_cross),
        CROSS + 2: (r.source, r.v_cross),
        CROSS + 3: (r.d_second, r.mixed_cross),
    }[kind]
    store_columns(*grad_place(r, kind), mm_tn(tokens(left), tokens(right)).astype(BF16))


AXES = ("y", "core", "z", "x")
SIZES = {"y": NY, "core": NC, "z": NZ, "x": NX}


class Place:
    def __init__(self, groups):
        d, t = lax.axis_index(DP), lax.axis_index(TENSOR)
        high, self.low = lax.div(d, groups), lax.rem(d, groups)
        self.groups = groups
        self.a, self.b = lax.div(high, NX), lax.rem(high, NX)
        self.y, self.c = lax.div(t, NC), lax.rem(t, NC)
        self.t = t

    def device(self, a=None, b=None, y=None, c=None):
        a, b = self.a if a is None else a, self.b if b is None else b
        y, c = self.y if y is None else y, self.c if c is None else c
        return ((a * NX + b) * self.groups + self.low, y * NC + c)

    def up(self, k):
        return lax.rem(self.a + k, NZ)

    def peer(self, axis, k=0):
        if axis == "z":
            return self.device(a=self.up(k))
        if axis == "x":
            return self.device(b=1 - self.b)
        if axis == "y":
            return self.device(y=1 - self.y)
        if axis == "core":
            return self.device(c=1 - self.c)
        return self.device(y=1 - self.y, c=1 - self.c)

    def region(self, fixed):
        return tuple(fixed[a] if a in fixed else slice(None) for a in AXES)

    def own(self, axes):
        place = {"y": self.y, "core": self.c, "z": self.a, "x": self.b}
        return {a: place[a] for a in axes}

    def others(self, axis):
        if axis == "z":
            return [self.up(k) for k in range(1, NZ)]
        return [{"y": 1 - self.y, "core": 1 - self.c, "x": 1 - self.b}[axis]]

    def peers(self, axis):
        if axis == "z":
            return [self.peer("z", k) for k in range(1, NZ)]
        return [self.peer(axis)]


class Link:
    def __init__(self, r):
        self.r = r
        self.used = 0
        self.all = []

    def slot(self):
        self.used += 1
        return self.used - 1

    def send(self, key, source, target, device):
        return pltpu.make_async_remote_copy(
            src_ref=source,
            dst_ref=target,
            send_sem=self.r.send_sems.at[key],
            recv_sem=self.r.recv_sems.at[key],
            device_id=device,
            device_id_type=MESH,
        )


class Stages:
    def __init__(self, link, counts):
        self.link = link
        self.keys = [[link.slot() for _ in range(n)] for n in counts]
        link.all.append(self)

    def start(self, stage):
        for copy in self.copies(stage):
            copy.start()

    def wait(self, stage):
        for copy in self.copies(stage):
            copy.wait_recv()

    def last(self):
        self.wait(len(self.keys) - 1)

    def turn(self, stage):
        self.wait(stage)
        self.start(stage + 1)

    def drain(self):
        for stage in range(len(self.keys)):
            for copy in self.copies(stage):
                copy.wait_send()


class Gather(Stages):
    def __init__(self, link, place, first, count, order):
        self.axes = (*order, "core")
        super().__init__(link, [SIZES[a] - 1 for a in self.axes])
        self.p, self.kinds = place, pl.ds(first, count)

    def copies(self, stage):
        p, link = self.p, self.link
        region = p.region(p.own(self.axes[stage:]))
        ref = link.r.w.at[(self.kinds, *region)]
        peers = p.peers(self.axes[stage])
        return [link.send(key, ref, ref, peer) for key, peer in zip(self.keys[stage], peers)]


class GatherNorms(Stages):
    def __init__(self, link, place):
        super().__init__(link, (NZ - 1, 1))
        self.p = place

    def copies(self, stage):
        p, pack, send = self.p, self.link.r.pack, self.link.send
        keys = self.keys[stage]
        if stage == 0:
            ref = pack.at[p.a, p.b]
            return [send(keys[k - 1], ref, ref, p.peer("z", k)) for k in range(1, NZ)]
        ref = pack.at[:, p.b]
        return [send(keys[0], ref, ref, p.peer("x"))]


class Scatter(Stages):
    def __init__(self, link, place, first, count, order, boxes):
        self.axes = ("core", *order)
        super().__init__(link, [SIZES[a] - 1 for a in self.axes])
        self.p, self.count, self.boxes = place, count, boxes
        self.ref, self.first = grad_place(link.r, first)

    def copies(self, stage):
        p, link = self.p, self.link
        axis, kept = self.axes[stage], p.own(self.axes[:stage])
        peers, others = p.peers(axis), p.others(axis)
        out = []
        for i, key in enumerate(self.keys[stage]):
            region = p.region({**kept, axis: others[i]})
            source = self.ref.at[(pl.ds(self.first, self.count), *region)]
            out.append(link.send(key, source, self.boxes[stage].at[i], peers[i]))
        return out

    def summed(self, stage, k):
        at = (self.first + k, *self.p.region(self.p.own(self.axes[: stage + 1])))
        box = self.boxes[stage]
        if box.shape[0] == 1:
            return at, self.ref[at].astype(F32) + box[0, k].astype(F32)
        total = self.ref[at].astype(F32)
        for i in range(box.shape[0]):
            total = total + box[i, k].astype(F32)
        return at, total

    def turn(self, stage):
        if stage == len(self.keys) - 1:
            self.share.go()
            return
        self.wait(stage)
        for k in range(self.count):
            at, total = self.summed(stage, k)
            self.ref[at] = total.astype(BF16)
        self.start(stage + 1)

    def total(self, k):
        return self.summed(len(self.keys) - 1, k)[1]


def box_name(name, stage):
    return "box_%d_%d" % (name, stage)


def scatter_boxes(name, count, order):
    out, axes = [], ("core", *order)
    for i, axis in enumerate(axes):
        free = [SIZES[a] for a in AXES if a not in axes[: i + 1]]
        shape = (SIZES[axis] - 1, count, *free, 64, 128)
        out.append((box_name(name, i), pltpu.VMEM(shape, BF16)))
    return out


Q, K, V, O, C0, C1, F0, F1, F2, F3 = range(10)
SUM, ROWS = 10, 20
(
    START, SELF_FORWARD, NORM_FORWARD, CROSS_FORWARD, FEED_FORWARD, FEED_BACK,
    FEED_GRAD, NORM_BACK, CROSS_BACK, GRAD, SELF_BACK, TAIL,
) = range(12)
GATHERS = {
    Q: (SELF, 1, "zxy"),
    K: (SELF + 1, 1, "zyx"),
    V: (SELF + 2, 1, "yzx"),
    O: (SELF + 3, 1, "zxy"),
    C0: (CROSS, 2, "zxy"),
    C1: (CROSS + 2, 2, "zyx"),
    F0: (FEED, 2, "yzx"),
    F1: (FEED + 2, 2, "xzy"),
    F2: (FEED + 4, 2, "yxz"),
    F3: (FEED + 6, 2, "zyx"),
}
SCATTERS = {
    F0: (FEED, 2, "zxy"),
    F1: (FEED + 2, 2, "yxz"),
    F2: (FEED + 4, 2, "yxz"),
    F3: (FEED + 6, 2, "zxy"),
    C0: (CROSS, 2, "yxz"),
    C1: (CROSS + 2, 2, "xzy"),
    O: (SELF + 3, 1, "zyx"),
    Q: (SELF, 1, "xyz"),
    K: (SELF + 1, 1, "zyx"),
    V: (SELF + 2, 1, "xzy"),
}
LATE = 2
PLAN = {
    (START, 0): ((K, -1), (F1, -1), (F2, -1), (Q, -1), (F2, 0), (C0, -1), (K, 0), (O, -1), (Q, 0),),
    (START, 1): ((V, -1), (C1, -1), (C0, 0), (K, 1), (V, 0), (Q, 1), (F0, -1), (F0, 0), (C1, 0),),
    (START, 2): ((O, 0), (C0, 1), (V, 1), (O, 1), (F1, 0), (Q, 2), (C1, 1), (F3, -1), (V, 2), (K, 2),),
    (SELF_FORWARD, 3): ((F0, 1), (O, 2),),
    (NORM_FORWARD, 0): ((C1, 2), (F2, 1), (C0, 2),),
    (NORM_FORWARD, 1): ((F3, 0),),
    (CROSS_FORWARD, 0): ((F1, 1),),
    (CROSS_FORWARD, 2): ((F3, 1),),
    (CROSS_FORWARD, 3): ((F0, 2),),
    (FEED_FORWARD, 0): ((F1, 2),),
    (FEED_FORWARD, 2): ((F2, 2),),
    (FEED_FORWARD, 3): ((F3, 2),),
    (FEED_BACK, 2): ((SUM + F0, 0),),
    (FEED_BACK, 3): ((SUM + F1, 0),),
    (NORM_BACK, 0): ((SUM + F2, 0),),
    (CROSS_BACK, 0): ((SUM + F3, 0),),
    (CROSS_BACK, 2): ((ROWS + 0, 0),),
    (GRAD, SELF + 3): ((SUM + F2, 1), (SUM + F1, 1), (ROWS + 1, 0),),
    (SELF_BACK, 0): ((ROWS + 2, 0), (ROWS + 3, 0), (SUM + F0, 1),),
    (SELF_BACK, 1): ((SUM + O, 0),),
    (GRAD, SELF + 2): ((SUM + F2, 2), (SUM + F3, 1),),
    (GRAD, CROSS): ((SUM + V, 0), (SUM + F1, 2),),
    (GRAD, CROSS + 3): ((SUM + F0, 2), (SUM + Q, 0),),
    (TAIL, 0): ((SUM + F3, 2), (SUM + K, 0), (SUM + C0, 0), (SUM + V, 1), (SUM + C1, 0), (SUM + C1, 1), (SUM + V, 2), (SUM + Q, 1), (SUM + K, 1), (SUM + F0, 3),),
    (TAIL, 1): ((SUM + C0, 1), (SUM + F3, 3), (SUM + F1, 3), (SUM + Q, 2), (SUM + O, 1), (SUM + C0, 2), (SUM + F2, 3), (SUM + C1, 2), (SUM + O, 2), (SUM + K, 2),),
}


class ScatterNorms(Stages):
    def __init__(self, link, place):
        super().__init__(link, (1, 1, 1, NZ - 1))
        self.p = place

    def copies(self, stage):
        p, r, send, keys = self.p, self.link.r, self.link.send, self.keys[stage]
        if stage == 0:
            return [send(keys[0], r.g_norm, r.n_box0, p.peer("core"))]
        if stage == 1:
            return [send(keys[0], r.n_box0, r.n_box1, p.peer("y"))]
        if stage == 2:
            return [send(keys[0], r.n_box1.at[:, 1 - p.b], r.n_box2, p.peer("x"))]
        return [
            send(keys[k - 1], r.n_box2.at[p.up(k)], r.n_box3.at[k - 1], p.peer("z", k))
            for k in range(1, NZ)
        ]

    def step(self, stage):
        p, r = self.p, self.link.r
        self.wait(stage)
        if stage == 0:
            r.n_box0[...] = r.g_norm[...] + r.n_box0[...]
        elif stage == 1:
            r.n_box1[...] = r.n_box0[...] + r.n_box1[...]
        else:
            r.n_box2[...] = r.n_box1[:, p.b] + r.n_box2[...]
        self.start(stage + 1)

    def total(self):
        r = self.link.r
        return r.n_box2[self.p.a] + ((r.n_box3[0] + r.n_box3[1]) + r.n_box3[2])


class ScatterEncoder(Stages):
    def __init__(self, link, place, share, micro):
        super().__init__(link, (NY * micro, micro))
        self.p, self.share, self.micro = place, share, micro
        self.boxes = (link.r.d_third, link.r.second_low)

    def rows(self, m, y, c):
        at = pl.multiple_of((y * NC + c) * self.share, self.share)
        return self.link.r.big1.at[m, pl.ds(at, self.share), :]

    def one(self, stage, m):
        p, r, send = self.p, self.link.r, self.link.send
        key = self.keys[stage][0]
        if stage == 0:
            return [
                send(
                    key + NY * m + y,
                    self.rows(m, y, 1 - p.c),
                    self.boxes[y].at[m],
                    p.peer("core"),
                )
                for y in range(NY)
            ]
        return [send(key + m, self.rows(m, 1 - p.y, p.c), r.e_box1.at[m], p.peer("y"))]

    def copies(self, stage):
        return [copy for m in range(self.micro) for copy in self.one(stage, m)]

    def begin(self, m):
        for copy in self.one(0, m):
            copy.start()

    def step(self, m):
        for copy in self.one(0, m):
            copy.wait_recv()
        for y in range(NY):
            ref = self.rows(m, y, self.p.c)
            ref[...] = ref[...] + self.boxes[y][m]
        for copy in self.one(1, m):
            copy.start()

    def finish(self):
        self.wait(1)
        for m in range(self.micro):
            ref = self.rows(m, self.p.y, self.p.c)
            ref[...] = ref[...] + self.link.r.e_box1[m]


class EncoderPart:
    def __init__(self, rows, m):
        self.rows, self.m = rows, m

    def turn(self, stage):
        self.rows.step(self.m)


class ShareFfn(Stages):
    def __init__(self, link, place, box, first, item):
        super().__init__(link, (3,))
        self.p, self.box, self.first, self.item = place, box, first, item

    def copies(self, stage):
        p, send, keys = self.p, self.link.send, self.keys[0]
        ref = self.box.at[p.t, pl.ds(self.first, self.item.count)]
        axes = ("core", "y", "both")
        return [send(keys[i], ref, ref, p.peer(axes[i])) for i in range(3)]

    def go(self):
        self.item.last()
        for k in range(self.item.count):
            self.box[self.p.t, self.first + k] = self.item.total(k).astype(BF16)
        self.start(0)


def each(count, body, ticks=None):
    def step(i, carry):
        for k, tick in (ticks or {}).items():
            pl.when(i == k)(tick)
        body(i)
        return carry

    lax.fori_loop(0, count, step, 0)


SEMS = 160


def layer_kernel(names, groups, scale, *refs):
    r = Refs()
    for name, ref in zip(names, refs):
        setattr(r, name, ref)
    micro, r.share = r.stream.shape[0], r.stream.shape[1]
    r.slots = r.share // SLOT
    r.quads = r.stream.shape[2] // QUAD
    r.enc_len = r.encoder.shape[1]
    r.frame = frame_rows(r.share)
    r.halves = micro // PIECE
    p = Place(groups)
    link = Link(r)

    mine = pl.ds(pl.multiple_of(p.t * r.share, r.share), r.share)
    half = pl.ds(pl.multiple_of(p.t * (r.share // 2), r.share // 2), r.share // 2)
    pairs = [
        (r.self_query, r.w.at[SELF, p.y, p.c, p.a, p.b]),
        (r.self_key_value, r.w.at[pl.ds(SELF + 1, 2), p.y, p.c, p.a, p.b]),
        (r.cross_query, r.w.at[CROSS, p.y, p.c, p.a, p.b]),
        (r.cross_key_value, r.w.at[pl.ds(CROSS + 1, 2), p.y, p.c, p.a, p.b]),
        (r.self_output, r.w.at[SELF + 3, p.y, p.c, p.a, p.b]),
        (r.cross_output, r.w.at[CROSS + 3, p.y, p.c, p.a, p.b]),
    ]
    down = pl.ds(pl.multiple_of(p.t * 128, 128), 128)
    for j in range(4):
        pairs.append(
            (
                r.ffn_out.at[pl.ds(j * 64, 64), down],
                r.w.at[FEED + 2 * j + 1, p.y, p.c, p.a, p.b],
            )
        )
    up = pl.ds(pl.multiple_of(p.t * 512, 512), 512)
    pairs.append((r.ffn_in.at[:, up], r.own_up))
    weights = len(pairs)
    pairs += [
        (r.stream_hbm.at[:, mine, :], r.stream),
        (r.context_hbm.at[:, mine, :], r.context),
        (r.masks_hbm.at[:, half, :], r.masks),
        (r.encoder, r.big1),
        (r.out_grad, r.cotangent),
    ]
    copies = [
        pltpu.make_async_copy(source, target, r.sems.at[i])
        for i, (source, target) in enumerate(pairs)
    ]
    for copy in copies:
        copy.start()
    partners = [p.peer("z", k) for k in range(1, NZ)]
    partners += [p.peer(axis) for axis in ("x", "y", "core", "both")]
    barrier = pltpu.get_barrier_semaphore()
    for device in partners:
        pl.semaphore_signal(barrier, inc=1, device_id=device, device_id_type=MESH)
    r.pack[p.a, p.b, 0:3, :64] = r.norm_gain[...].astype(F32)
    r.pack[p.a, p.b, 3:6, :64] = r.norm_bias[...].astype(F32)
    for copy in copies[:weights]:
        copy.wait()
    for j in range(4):
        at = j * 64
        r.w[FEED + 2 * j, p.y, p.c, p.a, p.b] = jnp.concatenate(
            [r.own_up[:, at : at + 64], r.own_up[:, 256 + at : 320 + at]], axis=1
        )
    pl.semaphore_wait(barrier, len(partners))

    chains = {name: Gather(link, p, *spec) for name, spec in GATHERS.items()}
    norms = GatherNorms(link, p)

    def run(phase, step):
        for name, stage in PLAN.get((phase, step), ()):
            if stage < 0:
                chains[name].start(0)
            else:
                chains[name].turn(stage)

    def loop(phase, count, body, needs=None):
        ticks = {}
        for i in range(count):
            names = (needs or {}).get(i, ())
            if PLAN.get((phase, i)) or names:

                def tick(i=i, names=names):
                    run(phase, i)
                    for name in names:
                        chains[name].last()

                ticks[i] = tick
        each(count, functools.partial(body, r), ticks)

    r.sums[...] = jnp.zeros(r.sums.shape, F32)
    run(START, 0)
    norms.start(0)
    run(START, 1)
    norms.wait(0)
    norms.start(1)
    for copy in copies[weights:]:
        copy.wait()
    run(START, 2)
    for name in (Q, K, V):
        chains[name].last()
    loop(SELF_FORWARD, micro, forward_self)
    norms.wait(1)
    r.norms[...] = jnp.concatenate(
        [r.pack[d // NX, d % NX, :, :64] for d in range(NZ * NX)], axis=1
    )
    loop(NORM_FORWARD, micro, first_norm, {0: (O,)})
    loop(CROSS_FORWARD, micro, forward_cross, {0: (C0, C1)})
    loop(FEED_FORWARD, 4 * r.halves, feed, {j * r.halves: (F0 + j,) for j in range(4)})
    for item in link.all:
        item.drain()
    link.all = []
    each(micro, functools.partial(third_norm, r))
    out = [pltpu.make_async_copy(r.d_first, r.block_out, r.sems.at[0])]
    out[0].start()

    sums = {}
    for name, spec in SCATTERS.items():
        boxes = [getattr(r, box_name(name, i)) for i in range(1 + len(spec[2]))]
        sums[name] = Scatter(link, p, *spec, boxes)
        if name >= F0:
            sums[name].share = ShareFfn(link, p, r.all_ffn, 2 * (name - F0), sums[name])
    norm_sums = ScatterNorms(link, p)
    rows = ScatterEncoder(link, p, r.share, micro)
    chains = {SUM + name: item for name, item in sums.items()}
    for m in range(micro):
        chains[ROWS + m] = EncoderPart(rows, m)

    def feed_both(j):
        for i in range(4):
            pl.when(j == i)(functools.partial(run, FEED_BACK, i))
        feed_back(r, j)
        for i in range(4):
            pl.when(j == i)(functools.partial(run, FEED_GRAD, i))
        feed_grad(r, j)
        for i in range(4):
            pl.when(j == i)(functools.partial(sums[F0 + i].start, 0))

    each(4, feed_both)
    run(NORM_BACK, 0)
    each(micro, functools.partial(second_back, r))
    clear_pads(r)
    out[0].wait()

    def cross_back(r, m):
        backward_cross(r, m)
        rows.begin(m)

    loop(CROSS_BACK, micro, cross_back)
    for d in range(NZ * NX):
        r.g_norm[d // NX, d % NX] = jnp.zeros(r.g_norm.shape[2:], F32)
        r.g_norm[d // NX, d % NX, :, :64] = r.sums[:, d * 64 : (d + 1) * 64]
    norm_sums.start(0)

    def grad(kind):
        run(GRAD, kind)
        weight_grad(r, kind)

    def cross_grads(pair):
        for k in (2 * pair, 2 * pair + 1):
            grad(CROSS + k)
        sums[C0 + pair].start(0)

    for pair in range(2 - LATE):
        cross_grads(pair)
    norm_sums.step(0)
    grad(SELF + 3)
    sums[O].start(0)
    norm_sums.step(1)
    loop(SELF_BACK, micro, backward_self)
    out = [
        pltpu.make_async_copy(r.cotangent, r.stream_grad, r.sems.at[0]),
        pltpu.make_async_copy(r.second_low, r.context_grad, r.sems.at[1]),
    ]
    for copy in out:
        copy.start()
    norm_sums.step(2)
    for name, kind in ((V, SELF + 2), (Q, SELF), (K, SELF + 1)):
        grad(kind)
        sums[name].start(0)
    for pair in range(2 - LATE, 2):
        cross_grads(pair)
    run(TAIL, 0)
    rows.finish()
    mine = pl.ds(pl.multiple_of(p.t * r.share, r.share), r.share)
    out.append(pltpu.make_async_copy(r.big1.at[:, mine, :], r.encoder_grad, r.sems.at[2]))
    out[2].start()
    run(TAIL, 1)
    for j in range(4):
        sums[F0 + j].share.wait(0)
    for t in range(NY * NC):
        halves = [
            r.all_ffn[t, 2 * j, :, h * 64 : (h + 1) * 64] for h in range(2) for j in range(4)
        ]
        r.grad_ffn_in[:, t * 512 : (t + 1) * 512] = (
            jnp.concatenate(halves, axis=1).astype(F32) * scale
        )
        for j in range(4):
            r.grad_ffn_out[j * 64 : (j + 1) * 64, t * 128 : (t + 1) * 128] = (
                r.all_ffn[t, 2 * j + 1].astype(F32) * scale
            )
    norm_sums.wait(3)
    total = norm_sums.total() * scale
    r.grad_norm_gain[...] = total[0:3, :64]
    r.grad_norm_bias[...] = total[3:6, :64]
    for name in (C0, C1, O, Q, K, V):
        sums[name].last()
    r.grad_cross_query[...] = sums[C0].total(0) * scale
    r.grad_cross_key_value[0] = sums[C0].total(1) * scale
    r.grad_cross_key_value[1] = sums[C1].total(0) * scale
    r.grad_cross_output[...] = sums[C1].total(1) * scale
    r.grad_self_output[...] = sums[O].total(0) * scale
    r.grad_self_query[...] = sums[Q].total(0) * scale
    r.grad_self_key_value[0] = sums[K].total(0) * scale
    r.grad_self_key_value[1] = sums[V].total(0) * scale
    for item in link.all:
        item.drain()
    for copy in out:
        copy.wait()


def vmem():
    return pl.BlockSpec(memory_space=pltpu.VMEM)


def hbm():
    return pl.BlockSpec(memory_space=pl.ANY)


WEIGHTS = (
    "self_query", "self_key_value", "self_output",
    "cross_query", "cross_key_value", "cross_output",
    "ffn_in", "ffn_out", "norm_gain", "norm_bias",
)


def layer(groups, scale, stream, context, encoder, masks, table, out_grad, weights):
    micro, row, width = stream.shape
    share = out_grad.shape[1]
    enc_len = encoder.shape[1]
    frame, wide = frame_rows(share), window_rows()
    slots, quads = share // SLOT, width // QUAD
    small = ("norm_gain", "norm_bias")
    ins = [
        ("stream_hbm", stream, hbm()),
        ("context_hbm", context, hbm()),
        ("encoder", encoder, hbm()),
        ("masks_hbm", masks, hbm()),
        ("table", table, pl.BlockSpec(memory_space=pltpu.SMEM)),
        ("out_grad", out_grad, hbm()),
    ]
    for name, value in zip(WEIGHTS, weights):
        ins.append((name, value, vmem() if name in small else hbm()))
    part = jax.ShapeDtypeStruct((micro, share, width), BF16)
    outs = [
        ("block_out", part, hbm()),
        ("stream_grad", part, hbm()),
        ("context_grad", part, hbm()),
        ("encoder_grad", part, hbm()),
    ]
    for name, value in zip(WEIGHTS, weights):
        outs.append(("grad_" + name, jax.ShapeDtypeStruct(value.shape, F32), vmem()))
    low = pltpu.VMEM((micro, share, width), BF16)
    high = pltpu.VMEM((micro, share, width), F32)
    window = pltpu.VMEM((micro, frame, width), BF16)
    big = pltpu.VMEM((micro, enc_len, width), BF16)
    norm = pltpu.VMEM((NZ, NX, 8, 128), F32)
    scratch = [
        ("w", pltpu.VMEM((KINDS, NY, NC, NZ, NX, 64, 128), BF16)),
        ("g_ffn", pltpu.VMEM((8, NY, NC, NZ, NX, 64, 128), BF16)),
        ("stream", low),
        ("context", low),
        ("cotangent", low),
        ("masks", pltpu.VMEM((micro, share // 2, 128), jnp.int32)),
        ("q_self", low),
        ("k_self", low),
        ("v_self", low),
        ("mixed_self", low),
        ("first_low", low),
        ("q_cross", low),
        ("k_cross", window),
        ("v_cross", window),
        ("source", window),
        ("mixed_cross", low),
        ("second_low", low),
        ("d_third", low),
        ("d_second", low),
        ("d_first", low),
        ("p_self", pltpu.VMEM((micro, slots, quads, SLOT, QUAD), BF16)),
        ("p_cross", pltpu.VMEM((micro, slots, quads, wide, QUAD), BF16)),
        ("residual", high),
        ("normed1", low),
        ("normed2", low),
        ("factor", pltpu.VMEM((micro, share, 2), F32)),
        ("big1", big),
        ("big2", big),
        ("own_up", pltpu.VMEM((64, 512), BF16)),
        ("norms", pltpu.VMEM((8, width), F32)),
        ("sums", pltpu.VMEM((8, width), F32)),
        ("pack", norm),
        ("g_norm", norm),
        ("n_box0", norm),
        ("n_box1", norm),
        ("n_box2", pltpu.VMEM((NZ, 8, 128), F32)),
        ("n_box3", pltpu.VMEM((NZ - 1, 8, 128), F32)),
        ("e_box1", low),
        ("all_ffn", pltpu.VMEM((NY * NC, 8, 64, 128), BF16)),
        ("sems", pltpu.SemaphoreType.DMA((19,))),
        ("send_sems", pltpu.SemaphoreType.DMA((SEMS,))),
        ("recv_sems", pltpu.SemaphoreType.DMA((SEMS,))),
    ]
    for name, (_, count, order) in SCATTERS.items():
        scratch += scatter_boxes(name, count, order)
    names = [item[0] for item in ins + outs + scratch]
    return pl.pallas_call(
        functools.partial(layer_kernel, names, groups, scale),
        out_shape=[item[1] for item in outs],
        in_specs=[item[2] for item in ins],
        out_specs=[item[2] for item in outs],
        scratch_shapes=[item[1] for item in scratch],
        compiler_params=pltpu.CompilerParams(
            vmem_limit_bytes=VMEM_LIMIT, collective_id=0, has_side_effects=True
        ),
        cost_estimate=pl.CostEstimate(
            flops=30_000_000_000, bytes_accessed=30_000_000, transcendentals=4_000_000
        ),
    )(*[item[1] for item in ins])


def copy_kernel(count, *refs):
    given, results, held = (refs[i * count : (i + 1) * count] for i in range(3))
    sems = refs[3 * count]
    loads = [pltpu.make_async_copy(a, b, sems.at[0, i]) for i, (a, b) in enumerate(zip(given, held))]
    stores = [
        pltpu.make_async_copy(a, b, sems.at[1, i]) for i, (a, b) in enumerate(zip(held, results))
    ]
    for load in loads:
        load.start()
    for load, store in zip(loads, stores):
        load.wait()
        store.start()
    for store in stores:
        store.wait()


def copy_all(values):
    count = len(values)
    return pl.pallas_call(
        functools.partial(copy_kernel, count),
        out_shape=[jax.ShapeDtypeStruct(v.shape, v.dtype) for v in values],
        in_specs=[hbm()] * count,
        out_specs=[hbm()] * count,
        scratch_shapes=[pltpu.VMEM(v.shape, v.dtype) for v in values]
        + [pltpu.SemaphoreType.DMA((2, count))],
        compiler_params=pltpu.CompilerParams(vmem_limit_bytes=VMEM_LIMIT),
    )(*values)


GATHER_DIM = (0, 1, 0, 0, 1, 0, 0, 0, 1, 1)


def per_device(
    query_stream,
    context_stream,
    encoder_out,
    query_masks,
    source_segments,
    out_grad,
    *weights,
):
    micro, row, width = query_stream.shape
    share = out_grad.shape[1]
    slots = share // SLOT
    t = lax.axis_index(TENSOR)
    replicas = lax.axis_size(DP)
    scale = float(micro * row * replicas) ** (-0.5)
    groups = replicas // (NZ * NX)
    weights = [item.T if i in (2, 5) else item for i, item in enumerate(weights)]
    near = [[i * groups + j for j in range(groups)] for i in range(NZ * NX)]
    if groups > 1:
        weights = [
            lax.all_gather(item, DP, axis=dim, tiled=True, axis_index_groups=near)
            for item, dim in zip(weights, GATHER_DIM)
        ]
    bounds = t * slots + jnp.arange(slots + 1, dtype=jnp.int32)
    starts = jnp.sum(
        (source_segments < bounds[None, :, None]).astype(jnp.int32), axis=-1
    )
    table = window_table(starts, share, encoder_out.shape[1])
    results = layer(
        groups, scale, query_stream, context_stream, encoder_out, query_masks, table,
        out_grad, weights,
    )
    results = copy_all(results)
    grads = results[4:]
    if groups > 1:
        grads = [
            lax.psum_scatter(
                item, DP, scatter_dimension=dim, tiled=True, axis_index_groups=near
            )
            for item, dim in zip(grads, GATHER_DIM)
        ]
    grads = [item.T if i in (2, 5) else item for i, item in enumerate(grads)]
    return (*results[:4], *grads)


def solution(mesh):
    in_specs = (
        P(None, DP, None),
        P(None, DP, None),
        P(None, DP, None),
        P(None, DP, None),
        P(None, DP, None),
        P(None, (DP, TENSOR), None),
        P(DP, TENSOR),
        P(None, DP, TENSOR),
        P(TENSOR, DP),
        P(DP, TENSOR),
        P(None, DP, TENSOR),
        P(TENSOR, DP),
        P(DP, None),
        P(DP, None),
        P(None, DP),
        P(None, DP),
    )
    out_specs = (
        P(None, (DP, TENSOR), None),
        P(None, (DP, TENSOR), None),
        P(None, (DP, TENSOR), None),
        P(None, (DP, TENSOR), None),
        P(DP, TENSOR),
        P(None, DP, TENSOR),
        P(TENSOR, DP),
        P(DP, TENSOR),
        P(None, DP, TENSOR),
        P(TENSOR, DP),
        P(DP, None),
        P(DP, None),
        P(None, DP),
        P(None, DP),
    )
    return jax.shard_map(
        per_device, mesh=mesh, in_specs=in_specs, out_specs=out_specs, check_vma=False
    )
```

time: 199 us -> 134 us (0.67)
  Pallas kernels: 177 us -> 130 us
  local copies, waits for them, and re-layouts: 19.6 us -> 1.68 us
    pallas_call x1, Pallas kernels: 177 us -> 126 us  [layer(): pl.pallas_call(functools.partial(layer_kernel, names, groups, scale), out...]
    unnamed x38 -> x4, local copies, waits for them, and re-layouts: 15.7 us -> 1 us
    pallas_call x0 -> x1, Pallas kernels: none -> 4.68 us  [copy_all(): pl.pallas_call(functools.partial(copy_kernel, count), out_shape=[jax.Shap...]
    pallas_call x2 -> x0, local copies, waits for them, and re-layouts: 3.22 us -> none  [layer(): pl.pallas_call(functools.partial(layer_kernel, names, groups, scale), out...]
where the time goes in v2:
time: 134 us; the launch traced here: 133 us
  Pallas kernels  130 us (97%)
  local copies, waits for them, and re-layouts  1.68 us (1%)
    pallas_call x1, Pallas kernels, layer(): pl.pallas_call(functools.partial(layer_kernel, names, groups, scale), out...  126 us
    pallas_call x1, Pallas kernels, copy_all(): pl.pallas_call(functools.partial(copy_kernel, count), out_shape=[jax.Shap...  4.68 us

profile of v2, /device:TPU:0, one launch (start us, length us, event | category | flops | bytes accessed | tf_op | source)
XLA Modules:
  0.0 133.3 jit_solution(767892988010570620)
XLA Ops:
  0.7 0.7 copy.38
  1.4 0.3 convert_reduce_fusion
  1.7 0.1 copy.36
  1.8 0.1 copy.34
  1.8 0.1 fusion.17
  2.0 0.1 copy.35
  2.1 0.1 add_select_fusion
  2.2 0.1 add_subtract_fusion
  2.2 0.7 concatenate.3.refs_4_
  2.9 125.6 %shard_map.263 = (bf16[4,256,512]{2,1,0:T(8,128)(2,1)}, bf16[4,256,512]{2,1,0:T(8,128)(2,1)}, bf16[4,256,512]{2,1,0:T(8,128)(2,1)}, bf16[4,256,512]{2,1,0:T(8,12...) custom-call(bf16[4,1024,512]{2,1,0:T(8,128)(2,1)} %refs_0_.1, ...), custom_call_target="tpu_custom_call" | custom-call | flops 30000001024 | bytes 30000000 | tf_op jit(solution)/shard_map/pallas_call | solution.py:1090
  128.5 4.7 %shard_map.264 = (bf16[4,256,512]{2,1,0:T(8,128)(2,1)}, bf16[4,256,512]{2,1,0:T(8,128)(2,1)}, bf16[4,256,512]{2,1,0:T(8,128)(2,1)}, bf16[4,256,512]{2,1,0:T(8,12...) custom-call(bf16[4,256,512]{2,1,0:T(8,128)(2,1)} %get-tuple-element., ...), custom_call_target="tpu_custom_call" | custom-call | tf_op jit(solution)/shard_map/pallas_call | solution.py:1123
  (4 shorter events, 0.0 us)

commit v3 on v2

--- a/solution.py
+++ b/solution.py
@@ -74,7 +74,7 @@
 
 def store_columns(ref, at, value):
     for t in range(NY * NC):
-        ref[at, t // NC, t % NC] = value[:, t * 128 : (t + 1) * 128].reshape(NZ, NX, -1, 128)
+        ref[at, t // NC, t % NC] = value[:, t * 128 : (t + 1) * 128].reshape(NZ // 2, 2, NX, -1, 128)
 
 
 def head_marks():
@@ -413,8 +413,13 @@
     store_columns(*grad_place(r, kind), mm_tn(tokens(left), tokens(right)).astype(BF16))
 
 
-AXES = ("y", "core", "z", "x")
-SIZES = {"y": NY, "core": NC, "z": NZ, "x": NX}
+AXES = ("y", "core", "p", "n", "x")
+SIZES = {"y": NY, "core": NC, "z": NZ, "p": NZ // 2, "n": 2, "x": NX, "w": NX * NY}
+JOINED = {"w": ("x", "y"), "z": ("p", "n")}
+
+
+def plain(axes):
+    return [part for axis in axes for part in JOINED.get(axis, (axis,))]
 
 
 class Place:
@@ -423,6 +428,7 @@
         high, self.low = lax.div(d, groups), lax.rem(d, groups)
         self.groups = groups
         self.a, self.b = lax.div(high, NX), lax.rem(high, NX)
+        self.a1, self.a0 = lax.div(self.a, 2), lax.rem(self.a, 2)
         self.y, self.c = lax.div(t, NC), lax.rem(t, NC)
         self.t = t
 
@@ -449,17 +455,28 @@
         return tuple(fixed[a] if a in fixed else slice(None) for a in AXES)
 
     def own(self, axes):
-        place = {"y": self.y, "core": self.c, "z": self.a, "x": self.b}
-        return {a: place[a] for a in axes}
+        place = {"y": self.y, "core": self.c, "p": self.a1, "n": self.a0, "x": self.b}
+        return {a: place[a] for a in plain(axes)}
 
     def others(self, axis):
         if axis == "z":
-            return [self.up(k) for k in range(1, NZ)]
-        return [{"y": 1 - self.y, "core": 1 - self.c, "x": 1 - self.b}[axis]]
+            ups = [self.up(k) for k in range(1, NZ)]
+            return [{"p": lax.div(up, 2), "n": lax.rem(up, 2)} for up in ups]
+        far = {axis: 1 - place for axis, place in self.own(AXES).items()}
+        if axis == "w":
+            x, y = far["x"], far["y"]
+            return [{"x": x, "y": self.y}, {"x": self.b, "y": y}, {"x": x, "y": y}]
+        return [{axis: far[axis]}]
 
     def peers(self, axis):
         if axis == "z":
             return [self.peer("z", k) for k in range(1, NZ)]
+        if axis == "w":
+            return [self.peer("x"), self.peer("y"), self.device(b=1 - self.b, y=1 - self.y)]
+        if axis == "p":
+            return [self.device(a=(1 - self.a1) * 2 + self.a0)]
+        if axis == "n":
+            return [self.device(a=self.a1 * 2 + 1 - self.a0)]
         return [self.peer(axis)]
 
 
@@ -553,7 +570,7 @@
         peers, others = p.peers(axis), p.others(axis)
         out = []
         for i, key in enumerate(self.keys[stage]):
-            region = p.region({**kept, axis: others[i]})
+            region = p.region({**kept, **others[i]})
             source = self.ref.at[(pl.ds(self.first, self.count), *region)]
             out.append(link.send(key, source, self.boxes[stage].at[i], peers[i]))
         return out
@@ -589,7 +606,7 @@
 def scatter_boxes(name, count, order):
     out, axes = [], ("core", *order)
     for i, axis in enumerate(axes):
-        free = [SIZES[a] for a in AXES if a not in axes[: i + 1]]
+        free = [SIZES[a] for a in AXES if a not in plain(axes[: i + 1])]
         shape = (SIZES[axis] - 1, count, *free, 64, 128)
         out.append((box_name(name, i), pltpu.VMEM(shape, BF16)))
     return out
@@ -602,56 +619,55 @@
     FEED_GRAD, NORM_BACK, CROSS_BACK, GRAD, SELF_BACK, TAIL,
 ) = range(12)
 GATHERS = {
-    Q: (SELF, 1, "zxy"),
-    K: (SELF + 1, 1, "zyx"),
+    Q: (SELF, 1, "pnw"),
+    K: (SELF + 1, 1, "pxny"),
     V: (SELF + 2, 1, "yzx"),
-    O: (SELF + 3, 1, "zxy"),
-    C0: (CROSS, 2, "zxy"),
-    C1: (CROSS + 2, 2, "zyx"),
-    F0: (FEED, 2, "yzx"),
-    F1: (FEED + 2, 2, "xzy"),
-    F2: (FEED + 4, 2, "yxz"),
-    F3: (FEED + 6, 2, "zyx"),
+    O: (SELF + 3, 1, "pxny"),
+    C0: (CROSS, 2, "pnyx"),
+    C1: (CROSS + 2, 2, "yxz"),
+    F0: (FEED, 2, "zw"),
+    F1: (FEED + 2, 2, "pnw"),
+    F2: (FEED + 4, 2, "xypn"),
+    F3: (FEED + 6, 2, "pynx"),
 }
 SCATTERS = {
-    F0: (FEED, 2, "zxy"),
-    F1: (FEED + 2, 2, "yxz"),
-    F2: (FEED + 4, 2, "yxz"),
-    F3: (FEED + 6, 2, "zxy"),
+    F0: (FEED, 2, "wz"),
+    F1: (FEED + 2, 2, "zxy"),
+    F2: (FEED + 4, 2, "xzy"),
+    F3: (FEED + 6, 2, "yxz"),
     C0: (CROSS, 2, "yxz"),
     C1: (CROSS + 2, 2, "xzy"),
-    O: (SELF + 3, 1, "zyx"),
-    Q: (SELF, 1, "xyz"),
-    K: (SELF + 1, 1, "zyx"),
-    V: (SELF + 2, 1, "xzy"),
+    O: (SELF + 3, 1, "xzy"),
+    Q: (SELF, 1, "xnyp"),
+    K: (SELF + 1, 1, "npw"),
+    V: (SELF + 2, 1, "zw"),
 }
 LATE = 2
 PLAN = {
-    (START, 0): ((K, -1), (F1, -1), (F2, -1), (Q, -1), (F2, 0), (C0, -1), (K, 0), (O, -1), (Q, 0),),
-    (START, 1): ((V, -1), (C1, -1), (C0, 0), (K, 1), (V, 0), (Q, 1), (F0, -1), (F0, 0), (C1, 0),),
-    (START, 2): ((O, 0), (C0, 1), (V, 1), (O, 1), (F1, 0), (Q, 2), (C1, 1), (F3, -1), (V, 2), (K, 2),),
-    (SELF_FORWARD, 3): ((F0, 1), (O, 2),),
-    (NORM_FORWARD, 0): ((C1, 2), (F2, 1), (C0, 2),),
-    (NORM_FORWARD, 1): ((F3, 0),),
+    (START, 0): ((C0, -1), (F2, -1), (C1, -1), (Q, -1), (K, -1), (V, -1), (V, 0), (O, -1), (C1, 0), (F3, -1),),
+    (START, 1): ((K, 0), (Q, 0), (F2, 0), (C0, 0), (K, 1), (O, 0), (F1, -1), (Q, 1), (F0, -1), (O, 1),),
+    (START, 2): ((C0, 1), (C1, 1), (Q, 2), (V, 1), (K, 2), (C0, 2), (O, 2), (K, 3), (F3, 0), (V, 2),),
+    (SELF_FORWARD, 1): ((O, 3), (F1, 0), (F0, 0),),
+    (SELF_FORWARD, 2): ((F2, 1),),
+    (SELF_FORWARD, 3): ((F3, 1), (C0, 3),),
+    (NORM_FORWARD, 0): ((C1, 2),),
     (CROSS_FORWARD, 0): ((F1, 1),),
-    (CROSS_FORWARD, 2): ((F3, 1),),
-    (CROSS_FORWARD, 3): ((F0, 2),),
+    (CROSS_FORWARD, 2): ((F2, 2), (F0, 1),),
+    (CROSS_FORWARD, 3): ((F3, 2),),
     (FEED_FORWARD, 0): ((F1, 2),),
-    (FEED_FORWARD, 2): ((F2, 2),),
-    (FEED_FORWARD, 3): ((F3, 2),),
-    (FEED_BACK, 2): ((SUM + F0, 0),),
+    (FEED_FORWARD, 2): ((F2, 3),),
+    (FEED_FORWARD, 4): ((F3, 3),),
+    (FEED_GRAD, 2): ((SUM + F0, 0),),
     (FEED_BACK, 3): ((SUM + F1, 0),),
-    (NORM_BACK, 0): ((SUM + F2, 0),),
-    (CROSS_BACK, 0): ((SUM + F3, 0),),
+    (CROSS_BACK, 0): ((SUM + F3, 0), (SUM + F2, 0),),
     (CROSS_BACK, 2): ((ROWS + 0, 0),),
-    (GRAD, SELF + 3): ((SUM + F2, 1), (SUM + F1, 1), (ROWS + 1, 0),),
-    (SELF_BACK, 0): ((ROWS + 2, 0), (ROWS + 3, 0), (SUM + F0, 1),),
-    (SELF_BACK, 1): ((SUM + O, 0),),
-    (GRAD, SELF + 2): ((SUM + F2, 2), (SUM + F3, 1),),
-    (GRAD, CROSS): ((SUM + V, 0), (SUM + F1, 2),),
-    (GRAD, CROSS + 3): ((SUM + F0, 2), (SUM + Q, 0),),
-    (TAIL, 0): ((SUM + F3, 2), (SUM + K, 0), (SUM + C0, 0), (SUM + V, 1), (SUM + C1, 0), (SUM + C1, 1), (SUM + V, 2), (SUM + Q, 1), (SUM + K, 1), (SUM + F0, 3),),
-    (TAIL, 1): ((SUM + C0, 1), (SUM + F3, 3), (SUM + F1, 3), (SUM + Q, 2), (SUM + O, 1), (SUM + C0, 2), (SUM + F2, 3), (SUM + C1, 2), (SUM + O, 2), (SUM + K, 2),),
+    (GRAD, SELF + 3): ((ROWS + 1, 0), (ROWS + 2, 0), (SUM + F0, 1), (SUM + F3, 1), (SUM + F2, 1), (SUM + F1, 1),),
+    (SELF_BACK, 0): ((ROWS + 3, 0),),
+    (SELF_BACK, 3): ((SUM + O, 0), (SUM + F3, 2),),
+    (GRAD, CROSS + 1): ((SUM + V, 0),),
+    (GRAD, CROSS + 2): ((SUM + K, 0), (SUM + Q, 0),),
+    (TAIL, 0): ((SUM + C0, 0), (SUM + C1, 0), (SUM + O, 1), (SUM + K, 1), (SUM + V, 1), (SUM + F0, 2), (SUM + F1, 2), (SUM + Q, 1), (SUM + C1, 1), (SUM + F2, 2),),
+    (TAIL, 1): ((SUM + C0, 1), (SUM + F3, 3), (SUM + Q, 2), (SUM + F1, 3), (SUM + K, 2), (SUM + F2, 3), (SUM + C0, 2), (SUM + O, 2), (SUM + Q, 3), (SUM + C1, 2),),
 }
 
 
@@ -773,7 +789,7 @@
     lax.fori_loop(0, count, step, 0)
 
 
-SEMS = 160
+SEMS = 180
 
 
 def layer_kernel(names, groups, scale, *refs):
@@ -792,19 +808,19 @@
     mine = pl.ds(pl.multiple_of(p.t * r.share, r.share), r.share)
     half = pl.ds(pl.multiple_of(p.t * (r.share // 2), r.share // 2), r.share // 2)
     pairs = [
-        (r.self_query, r.w.at[SELF, p.y, p.c, p.a, p.b]),
-        (r.self_key_value, r.w.at[pl.ds(SELF + 1, 2), p.y, p.c, p.a, p.b]),
-        (r.cross_query, r.w.at[CROSS, p.y, p.c, p.a, p.b]),
-        (r.cross_key_value, r.w.at[pl.ds(CROSS + 1, 2), p.y, p.c, p.a, p.b]),
-        (r.self_output, r.w.at[SELF + 3, p.y, p.c, p.a, p.b]),
-        (r.cross_output, r.w.at[CROSS + 3, p.y, p.c, p.a, p.b]),
+        (r.self_query, r.w.at[SELF, p.y, p.c, p.a1, p.a0, p.b]),
+        (r.self_key_value, r.w.at[pl.ds(SELF + 1, 2), p.y, p.c, p.a1, p.a0, p.b]),
+        (r.cross_query, r.w.at[CROSS, p.y, p.c, p.a1, p.a0, p.b]),
+        (r.cross_key_value, r.w.at[pl.ds(CROSS + 1, 2), p.y, p.c, p.a1, p.a0, p.b]),
+        (r.self_output, r.w.at[SELF + 3, p.y, p.c, p.a1, p.a0, p.b]),
+        (r.cross_output, r.w.at[CROSS + 3, p.y, p.c, p.a1, p.a0, p.b]),
     ]
     down = pl.ds(pl.multiple_of(p.t * 128, 128), 128)
     for j in range(4):
         pairs.append(
             (
                 r.ffn_out.at[pl.ds(j * 64, 64), down],
-                r.w.at[FEED + 2 * j + 1, p.y, p.c, p.a, p.b],
+                r.w.at[FEED + 2 * j + 1, p.y, p.c, p.a1, p.a0, p.b],
             )
         )
     up = pl.ds(pl.multiple_of(p.t * 512, 512), 512)
@@ -825,6 +841,7 @@
         copy.start()
     partners = [p.peer("z", k) for k in range(1, NZ)]
     partners += [p.peer(axis) for axis in ("x", "y", "core", "both")]
+    partners.append(p.device(b=1 - p.b, y=1 - p.y))
     barrier = pltpu.get_barrier_semaphore()
     for device in partners:
         pl.semaphore_signal(barrier, inc=1, device_id=device, device_id_type=MESH)
@@ -834,7 +851,7 @@
         copy.wait()
     for j in range(4):
         at = j * 64
-        r.w[FEED + 2 * j, p.y, p.c, p.a, p.b] = jnp.concatenate(
+        r.w[FEED + 2 * j, p.y, p.c, p.a1, p.a0, p.b] = jnp.concatenate(
             [r.own_up[:, at : at + 64], r.own_up[:, 256 + at : 320 + at]], axis=1
         )
     pl.semaphore_wait(barrier, len(partners))
@@ -867,11 +884,11 @@
     run(START, 0)
     norms.start(0)
     run(START, 1)
-    norms.wait(0)
-    norms.start(1)
     for copy in copies[weights:]:
         copy.wait()
     run(START, 2)
+    norms.wait(0)
+    norms.start(1)
     for name in (Q, K, V):
         chains[name].last()
     loop(SELF_FORWARD, micro, forward_self)
@@ -938,10 +955,9 @@
 
     for pair in range(2 - LATE):
         cross_grads(pair)
-    norm_sums.step(0)
     grad(SELF + 3)
     sums[O].start(0)
-    norm_sums.step(1)
+    norm_sums.step(0)
     loop(SELF_BACK, micro, backward_self)
     out = [
         pltpu.make_async_copy(r.cotangent, r.stream_grad, r.sems.at[0]),
@@ -949,13 +965,14 @@
     ]
     for copy in out:
         copy.start()
-    norm_sums.step(2)
     for name, kind in ((V, SELF + 2), (Q, SELF), (K, SELF + 1)):
         grad(kind)
         sums[name].start(0)
     for pair in range(2 - LATE, 2):
         cross_grads(pair)
+    norm_sums.step(1)
     run(TAIL, 0)
+    norm_sums.step(2)
     rows.finish()
     mine = pl.ds(pl.multiple_of(p.t * r.share, r.share), r.share)
     out.append(pltpu.make_async_copy(r.big1.at[:, mine, :], r.encoder_grad, r.sems.at[2]))
@@ -1041,8 +1058,8 @@
     big = pltpu.VMEM((micro, enc_len, width), BF16)
     norm = pltpu.VMEM((NZ, NX, 8, 128), F32)
     scratch = [
-        ("w", pltpu.VMEM((KINDS, NY, NC, NZ, NX, 64, 128), BF16)),
-        ("g_ffn", pltpu.VMEM((8, NY, NC, NZ, NX, 64, 128), BF16)),
+        ("w", pltpu.VMEM((KINDS, NY, NC, NZ // 2, 2, NX, 64, 128), BF16)),
+        ("g_ffn", pltpu.VMEM((8, NY, NC, NZ // 2, 2, NX, 64, 128), BF16)),
         ("stream", low),
         ("context", low),
         ("cotangent", low),

time: 134 us -> 131 us (0.978)
  Pallas kernels: 130 us -> 128 us
    pallas_call x1, Pallas kernels: 126 us -> 123 us  [layer(): pl.pallas_call(functools.partial(layer_kernel, names, groups, scale), out...]
where the time goes in v3:
time: 131 us
  Pallas kernels  128 us (98%)
  local copies, waits for them, and re-layouts  1.68 us (1%)
    pallas_call x1, Pallas kernels, layer(): pl.pallas_call(functools.partial(layer_kernel, names, groups, scale), out...  123 us
    pallas_call x1, Pallas kernels, copy_all(): pl.pallas_call(functools.partial(copy_kernel, count), out_shape=[jax.Shap...  4.68 us

profile of v3, /device:TPU:0, one launch (start us, length us, event | category | flops | bytes accessed | tf_op | source)
XLA Modules:
  0.0 130.7 jit_solution(13395179166521423807)
XLA Ops:
  0.7 0.7 copy.38
  1.4 0.3 convert_reduce_fusion
  1.7 0.1 copy.36
  1.8 0.1 copy.34
  1.8 0.1 fusion.17
  2.0 0.1 copy.35
  2.1 0.1 add_select_fusion
  2.2 0.1 add_subtract_fusion
  2.2 0.7 concatenate.3.refs_4_
  2.9 122.9 %shard_map.263 = (bf16[4,256,512]{2,1,0:T(8,128)(2,1)}, bf16[4,256,512]{2,1,0:T(8,128)(2,1)}, bf16[4,256,512]{2,1,0:T(8,128)(2,1)}, bf16[4,256,512]{2,1,0:T(8,12...) custom-call(bf16[4,1024,512]{2,1,0:T(8,128)(2,1)} %refs_0_.1, ...), custom_call_target="tpu_custom_call" | custom-call | flops 30000001024 | bytes 30000000 | tf_op jit(solution)/shard_map/pallas_call | solution.py:1107
  125.9 4.7 %shard_map.264 = (bf16[4,256,512]{2,1,0:T(8,128)(2,1)}, bf16[4,256,512]{2,1,0:T(8,128)(2,1)}, bf16[4,256,512]{2,1,0:T(8,128)(2,1)}, bf16[4,256,512]{2,1,0:T(8,12...) custom-call(bf16[4,256,512]{2,1,0:T(8,128)(2,1)} %get-tuple-element., ...), custom_call_target="tpu_custom_call" | custom-call | tf_op jit(solution)/shard_map/pallas_call | solution.py:1140
  (4 shorter events, 0.0 us)

commit v4 on v3

--- a/solution.py
+++ b/solution.py
@@ -260,11 +260,11 @@
     for at in range(0, 512, 256):
         inner = mm(low, up[:, at : at + 256])
         square = inner * inner
-        bent = jnp.tanh(gelu_coef * inner * (1.0 + gelu_cube * square))
-        half = 0.5 * (1.0 + bent)
-        r.big1[j, rows, at : at + 256] = (inner * half).astype(BF16)
-        slope = half + 0.5 * inner * (1.0 - bent * bent) * gelu_coef * (
-            1.0 + 3.0 * gelu_cube * square
+        half = 0.5 + 0.5 * jnp.tanh(inner * (gelu_coef + gelu_coef * gelu_cube * square))
+        hidden = inner * half
+        r.big1[j, rows, at : at + 256] = hidden.astype(BF16)
+        slope = half + hidden * (1.0 - half) * (
+            2.0 * gelu_coef + 6.0 * gelu_coef * gelu_cube * square
         )
         r.big2[j, rows, at : at + 256] = slope.astype(BF16)
     r.residual[some] += mm(r.big1[j, rows, :], down).reshape(PIECE, r.share, -1)
@@ -837,14 +837,14 @@
         pltpu.make_async_copy(source, target, r.sems.at[i])
         for i, (source, target) in enumerate(pairs)
     ]
-    for copy in copies:
-        copy.start()
     partners = [p.peer("z", k) for k in range(1, NZ)]
     partners += [p.peer(axis) for axis in ("x", "y", "core", "both")]
     partners.append(p.device(b=1 - p.b, y=1 - p.y))
     barrier = pltpu.get_barrier_semaphore()
     for device in partners:
         pl.semaphore_signal(barrier, inc=1, device_id=device, device_id_type=MESH)
+    for copy in copies[:weights]:
+        copy.start()
     r.pack[p.a, p.b, 0:3, :64] = r.norm_gain[...].astype(F32)
     r.pack[p.a, p.b, 3:6, :64] = r.norm_bias[...].astype(F32)
     for copy in copies[:weights]:
@@ -855,6 +855,8 @@
             [r.own_up[:, at : at + 64], r.own_up[:, 256 + at : 320 + at]], axis=1
         )
     pl.semaphore_wait(barrier, len(partners))
+    for copy in copies[weights:]:
+        copy.start()
 
     chains = {name: Gather(link, p, *spec) for name, spec in GATHERS.items()}
     norms = GatherNorms(link, p)
@@ -970,14 +972,14 @@
         sums[name].start(0)
     for pair in range(2 - LATE, 2):
         cross_grads(pair)
+    run(TAIL, 0)
     norm_sums.step(1)
-    run(TAIL, 0)
+    run(TAIL, 1)
     norm_sums.step(2)
     rows.finish()
     mine = pl.ds(pl.multiple_of(p.t * r.share, r.share), r.share)
     out.append(pltpu.make_async_copy(r.big1.at[:, mine, :], r.encoder_grad, r.sems.at[2]))
     out[2].start()
-    run(TAIL, 1)
     for j in range(4):
         sums[F0 + j].share.wait(0)
     for t in range(NY * NC):

time: 131 us -> 131 us (level)
  no operation moved by 1% of the time
where the time goes in v4:
time: 131 us; the launch traced here: 130 us
  Pallas kernels  127 us (97%)
  local copies, waits for them, and re-layouts  1.68 us (1%)
    pallas_call x1, Pallas kernels, layer(): pl.pallas_call(functools.partial(layer_kernel, names, groups, scale), out...  123 us
    pallas_call x1, Pallas kernels, copy_all(): pl.pallas_call(functools.partial(copy_kernel, count), out_shape=[jax.Shap...  4.68 us

profile of v4, /device:TPU:0, one launch (start us, length us, event | category | flops | bytes accessed | tf_op | source)
XLA Modules:
  0.0 130.4 jit_solution(3611431338493550332)
XLA Ops:
  0.7 0.7 copy.38
  1.4 0.3 convert_reduce_fusion
  1.7 0.1 copy.36
  1.8 0.1 copy.34
  1.8 0.1 fusion.17
  2.0 0.1 copy.35
  2.1 0.1 add_select_fusion
  2.2 0.1 add_subtract_fusion
  2.2 0.7 concatenate.3.refs_4_
  2.9 122.6 %shard_map.263 = (bf16[4,256,512]{2,1,0:T(8,128)(2,1)}, bf16[4,256,512]{2,1,0:T(8,128)(2,1)}, bf16[4,256,512]{2,1,0:T(8,128)(2,1)}, bf16[4,256,512]{2,1,0:T(8,12...) custom-call(bf16[4,1024,512]{2,1,0:T(8,128)(2,1)} %refs_0_.1, ...), custom_call_target="tpu_custom_call" | custom-call | flops 30000001024 | bytes 30000000 | tf_op jit(solution)/shard_map/pallas_call | solution.py:1109
  125.6 4.7 %shard_map.264 = (bf16[4,256,512]{2,1,0:T(8,128)(2,1)}, bf16[4,256,512]{2,1,0:T(8,128)(2,1)}, bf16[4,256,512]{2,1,0:T(8,128)(2,1)}, bf16[4,256,512]{2,1,0:T(8,12...) custom-call(bf16[4,256,512]{2,1,0:T(8,128)(2,1)} %get-tuple-element., ...), custom_call_target="tpu_custom_call" | custom-call | tf_op jit(solution)/shard_map/pallas_call | solution.py:1142
  (4 shorter events, 0.0 us)

commit v5 on v4

--- a/solution.py
+++ b/solution.py
@@ -591,8 +591,12 @@
             return
         self.wait(stage)
         for k in range(self.count):
-            at, total = self.summed(stage, k)
-            self.ref[at] = total.astype(BF16)
+            if self.boxes[stage].shape[0] == 1:
+                at = (self.first + k, *self.p.region(self.p.own(self.axes[: stage + 1])))
+                self.ref[at] = self.ref[at] + self.boxes[stage][0, k]
+            else:
+                at, total = self.summed(stage, k)
+                self.ref[at] = total.astype(BF16)
         self.start(stage + 1)
 
     def total(self, k):

time: 131 us -> 130 us (level)
  no operation moved by 1% of the time
where the time goes in v5:
time: 130 us
  Pallas kernels  127 us (98%)
  local copies, waits for them, and re-layouts  1.68 us (1%)
    pallas_call x1, Pallas kernels, layer(): pl.pallas_call(functools.partial(layer_kernel, names, groups, scale), out...  122 us
    pallas_call x1, Pallas kernels, copy_all(): pl.pallas_call(functools.partial(copy_kernel, count), out_shape=[jax.Shap...  4.68 us

profile of v5, /device:TPU:0, one launch (start us, length us, event | category | flops | bytes accessed | tf_op | source)
XLA Modules:
  0.0 130.1 jit_solution(17149663077411730549)
XLA Ops:
  0.7 0.7 copy.38
  1.4 0.3 convert_reduce_fusion
  1.7 0.1 copy.36
  1.8 0.1 copy.34
  1.8 0.1 fusion.17
  2.0 0.1 copy.35
  2.1 0.1 add_select_fusion
  2.2 0.1 add_subtract_fusion
  2.2 0.7 concatenate.3.refs_4_
  2.9 122.3 %shard_map.263 = (bf16[4,256,512]{2,1,0:T(8,128)(2,1)}, bf16[4,256,512]{2,1,0:T(8,128)(2,1)}, bf16[4,256,512]{2,1,0:T(8,128)(2,1)}, bf16[4,256,512]{2,1,0:T(8,12...) custom-call(bf16[4,1024,512]{2,1,0:T(8,128)(2,1)} %refs_0_.1, ...), custom_call_target="tpu_custom_call" | custom-call | flops 30000001024 | bytes 30000000 | tf_op jit(solution)/shard_map/pallas_call | solution.py:1113
  125.3 4.7 %shard_map.264 = (bf16[4,256,512]{2,1,0:T(8,128)(2,1)}, bf16[4,256,512]{2,1,0:T(8,128)(2,1)}, bf16[4,256,512]{2,1,0:T(8,128)(2,1)}, bf16[4,256,512]{2,1,0:T(8,12...) custom-call(bf16[4,256,512]{2,1,0:T(8,128)(2,1)} %get-tuple-element., ...), custom_call_target="tpu_custom_call" | custom-call | tf_op jit(solution)/shard_map/pallas_call | solution.py:1146
  (4 shorter events, 0.0 us)
